TPU v7x, 32 devices: a whole 2x2x4 slice. The times are simulated.
32 devices in a mesh: groups: 2 (over y), row: 16 (over z, x, core).
Axes of the slice: x: 2, y: 2, z: 4, core: 2. Of those that a mesh axis runs over, the one named last changes fastest.
Arguments:
- frontal: float32 [16384, 8192], P(('groups', 'row')), parts along dimension 0, may hold values from -8 to 192, as said below
- child_tiles: bfloat16 [2048, 128, 128], P(('groups', 'row')), parts along dimension 0, may hold values from -3 to 3
- child_rows: int32 [2048, 1], P(('groups', 'row')), parts along dimension 0, may hold values from 0 to 63; in each aligned block of 64 rows (0 to 63, 64 to 127, ...) at most 2 rows name the same one
- child_cols: int32 [2048], P(('groups', 'row')), parts along dimension 0, may hold values from 0 to 63
Outputs:
- factored: float32 [16384, 8192], P(('groups', 'row')), parts along dimension 0
There are 2 independent parts, one for each index of `groups`. A program takes and returns all parts, laid end to end along the dimension named above; each array names one. Nothing has to cross between parts.
Inputs may be any that keep to these rules, and one draw needn't show every extreme that they name: `frontal`: the leading square block of 256 rows and columns is symmetric and strongly diagonally dominant, so that it stays positive definite after the child tiles are added. `child_rows`: among the 64 tiles of one device no parent tile row is named by more than 2 of them; in every draw some device names some parent tile row exactly 2 times.
All inputs are finite; a program needn't handle non-finite values.
Results may differ from a plain program's by a relative error of at most 0.0003.
Values may be sent and summed in bfloat16 or wider, within the bound.
No kernel may reach another device: no remote copies, remote signals or barrier semaphores. Data moves between devices by JAX's collectives and lax.ppermute only.
A program may use at most 192 MiB of HBM per device.

v0:
```python
import functools
import jax
import jax.numpy as jnp
from jax import lax
from jax.experimental import pallas as pl
from jax.experimental.pallas import tpu as pltpu
from jax.sharding import PartitionSpec as P

MOST_SAME = 2
FIRST = 3
SECOND = 3
HEAD = 16
VMEM_LIMIT = 56 << 20


highest = lax.Precision.HIGHEST
f32, bf16 = jnp.float32, jnp.bfloat16


def loop(count, body):
    lax.fori_loop(0, count, lambda i, carry: (body(i), carry)[1], 0)


def pack_kernel(
    tile_rows, per_dev, rows_ref, cols_ref, tiles_ref, first_ref, second_ref, third_ref,
    heads, heads_out, counts, sems, head_sem,
):
    tiles, side, _ = tiles_ref.shape
    devices = first_ref.shape[0]
    lanes = lax.broadcasted_iota(jnp.int32, (8, 128), 1)
    subs = lax.broadcasted_iota(jnp.int32, (8, 128), 0)
    heads[...] = jnp.zeros_like(heads)

    def clear(d):
        counts[d] = 0

    loop(devices, clear)

    def place(i, wanted):
        row, col = rows_ref[i], cols_ref[i]

        @pl.when((col < 2) == wanted)
        def _():
            d, q = row // per_dev, row % per_dev
            s = counts[d]
            counts[d] = s + 1
            here = (lanes == s) & (subs == 0)
            heads[d] = jnp.where(here, (q * tile_rows + col + 1).astype(f32), heads[d])

            @pl.when(s < FIRST)
            def _():
                pltpu.make_async_copy(
                    tiles_ref.at[i], first_ref.at[d, pl.ds(s * side, side)], sems.at[i]
                ).start()

            @pl.when((s >= FIRST) & (s < FIRST + SECOND))
            def _():
                pltpu.make_async_copy(
                    tiles_ref.at[i], second_ref.at[d, pl.ds((s - FIRST) * side, side)], sems.at[i]
                ).start()

            @pl.when(s >= FIRST + SECOND)
            def _():
                pltpu.make_async_copy(
                    tiles_ref.at[i],
                    third_ref.at[d, pl.ds((s - FIRST - SECOND) * side, side)],
                    sems.at[i],
                ).start()

    def most():
        return lax.fori_loop(0, devices, lambda d, m: jnp.maximum(m, counts[d]), 0)

    loop(tiles, lambda i: place(i, True))
    lead_over = (most() > FIRST).astype(f32)
    loop(tiles, lambda i: place(i, False))
    over = (most() > FIRST + SECOND).astype(f32)
    flags = jnp.where(lanes == 0, lead_over, jnp.where(lanes == 1, over, 0.0))
    marked = jnp.where((subs == 1)[None], flags[None], heads[...])
    heads_out[...] = jnp.concatenate([marked, jnp.zeros_like(marked)], axis=1).astype(bf16)
    copy = pltpu.make_async_copy(heads_out, first_ref.at[:, pl.ds(FIRST * side, HEAD)], head_sem)
    copy.start()

    def finish(i):
        pltpu.make_async_copy(tiles_ref.at[i], first_ref.at[0, pl.ds(0, side)], sems.at[i]).wait()

    loop(tiles, finish)
    copy.wait()


def pack(child_tiles, child_rows, child_cols, devices, tile_rows):
    tiles, side, _ = child_tiles.shape
    per_dev = tile_rows // devices
    third = MOST_SAME * per_dev - FIRST - SECOND
    smem, anyw = (pl.BlockSpec(memory_space=m) for m in (pltpu.SMEM, pl.ANY))
    return pl.pallas_call(
        functools.partial(pack_kernel, tile_rows, per_dev),
        grid=(1,),
        out_shape=(
            jax.ShapeDtypeStruct((devices, FIRST * side + HEAD, side), bf16),
            jax.ShapeDtypeStruct((devices, SECOND * side, side), bf16),
            jax.ShapeDtypeStruct((devices, third * side, side), bf16),
        ),
        in_specs=[smem, smem, pl.BlockSpec((tiles, side, side), lambda i: (0, 0, 0))],
        out_specs=(anyw, anyw, anyw),
        scratch_shapes=[
            pltpu.VMEM((devices, 8, 128), f32),
            pltpu.VMEM((devices, HEAD, 128), bf16),
            pltpu.SMEM((devices,), jnp.int32),
            pltpu.SemaphoreType.DMA((tiles,)),
            pltpu.SemaphoreType.DMA,
        ],
        compiler_params=pltpu.CompilerParams(vmem_limit_bytes=VMEM_LIMIT),
        name="pack",
    )(child_rows[:, 0], child_cols, child_tiles)


def lead_kernel(tile_rows, slots, row_ref, labels_ref, front_ref, tiles_ref, out_ref, coded_ref):
    side = tiles_ref.shape[2]
    rows, lead = out_ref.shape
    out_ref[...] = front_ref[...]

    def body(n):
        d, s = n // FIRST, n % FIRST
        label = labels_ref[d * slots + s]
        q, col = label // tile_rows, label % tile_rows

        @pl.when((label >= 0) & (col < 2))
        def _():
            at = (pl.ds(pl.multiple_of(q * side, side), side),
                  pl.ds(pl.multiple_of(col * side, side), side))
            out_ref[at] = out_ref[at] + tiles_ref[d, pl.ds(pl.multiple_of(s * side, side), side)].astype(f32)

    loop(tiles_ref.shape[0] * FIRST, body)
    low, high = -32768.0, 32767.0
    turned = out_ref[...].T
    on = lax.broadcasted_iota(jnp.int32, turned.shape, 0) == lax.broadcasted_iota(jnp.int32, turned.shape, 1)
    diagonal = jnp.sum(jnp.where(on, turned, 0.0), axis=0, keepdims=True)
    turned = jnp.where(on & (row_ref[0] == 0), 0.0, turned)

    def power(most):
        return jnp.ceil(jnp.log2(jnp.maximum(most, 1e-30))) - 15.0

    scale = power(jnp.max(jnp.abs(turned), axis=0, keepdims=True))
    values = jnp.clip(jnp.round(turned * jnp.exp2(-scale)), low, high)
    coded_ref[0, :lead] = values.astype(jnp.int32).astype(jnp.int16)
    own = power(jnp.abs(diagonal))
    wide = diagonal * jnp.exp2(-own)
    upper = jnp.clip(jnp.round(wide), low, high)
    lower = jnp.clip(jnp.round((wide - upper) * 32768.0), low, high)
    subs = lax.broadcasted_iota(jnp.int32, (HEAD, rows), 0)
    head = jnp.zeros((HEAD, rows), f32)
    for i, value in enumerate((scale, own, upper, lower)):
        head = jnp.where(subs == i, value, head)
    coded_ref[0, lead:] = head.astype(jnp.int32).astype(jnp.int16)


def lead_columns(row, labels, frontal, arrived, tile_rows):
    rows = frontal.shape[0]
    lead = 2 * arrived.shape[2]
    smem = pl.BlockSpec(memory_space=pltpu.SMEM)
    return pl.pallas_call(
        functools.partial(lead_kernel, tile_rows, labels.shape[1]),
        grid=(1,),
        out_shape=(
            jax.ShapeDtypeStruct((rows, lead), f32),
            jax.ShapeDtypeStruct((1, lead + HEAD, rows), jnp.int16),
        ),
        in_specs=[
            smem, smem,
            pl.BlockSpec((rows, lead), lambda i: (0, 0)),
            pl.BlockSpec(arrived.shape, lambda i: (0, 0, 0)),
        ],
        out_specs=(
            pl.BlockSpec((rows, lead), lambda i: (0, 0)),
            pl.BlockSpec((1, lead + HEAD, rows), lambda i: (0, 0, 0)),
        ),
        compiler_params=pltpu.CompilerParams(vmem_limit_bytes=VMEM_LIMIT),
        name="lead_columns",
    )(row, labels.reshape(-1), frontal, arrived)


def place_kernel(tile_rows, labels_ref, owner_ref, tiles_ref, front_ref, out_ref, held, listed, in_sems, out_sems):
    side = tiles_ref.shape[2]
    slots = tiles_ref.shape[1] // side

    def spot(n):
        label = labels_ref[n]
        q, col = label // tile_rows, label % tile_rows
        return out_ref.at[pl.ds(pl.multiple_of(q * side, side), side), pl.ds(pl.multiple_of(col * side, side), side)]

    def fetch(n, used):
        listed[used] = n

        @pl.when(owner_ref[n] == n)
        def _():
            pltpu.make_async_copy(spot(n), held.at[n], in_sems.at[n]).start()

        return used + (labels_ref[n] >= 0).astype(jnp.int32)

    def add(i):
        n = listed[i]
        m = owner_ref[n]

        @pl.when(m == n)
        def _():
            pltpu.make_async_copy(spot(n), held.at[n], in_sems.at[n]).wait()

        held[m] += tiles_ref[n // slots, pl.ds(pl.multiple_of(n % slots * side, side), side)].astype(f32)

    def put(i):
        n = listed[i]

        @pl.when(owner_ref[n] == n)
        def _():
            pltpu.make_async_copy(held.at[n], spot(n), out_sems.at[n]).start()

    def finish(i):
        n = listed[i]

        @pl.when(owner_ref[n] == n)
        def _():
            pltpu.make_async_copy(held.at[n], spot(n), out_sems.at[n]).wait()

    used = lax.fori_loop(0, tiles_ref.shape[0] * slots, fetch, 0)
    for step in (add, put, finish):
        loop(used, step)


def place(front, labels, tiles, tile_rows):
    side = tiles.shape[2]
    labels = labels.reshape(-1)
    size = labels.size
    ids = jnp.arange(size, dtype=jnp.int32)
    owner = jnp.min(jnp.where(labels[:, None] == labels[None, :], ids[None, :], size), axis=1)
    owner = jnp.where(labels < 0, -1, owner)
    smem = pl.BlockSpec(memory_space=pltpu.SMEM)
    return pl.pallas_call(
        functools.partial(place_kernel, tile_rows),
        grid=(1,),
        out_shape=jax.ShapeDtypeStruct(front.shape, f32),
        in_specs=[smem, smem, pl.BlockSpec(tiles.shape, lambda i: (0, 0, 0)), pl.BlockSpec(memory_space=pl.ANY)],
        out_specs=pl.BlockSpec(memory_space=pl.ANY),
        input_output_aliases={3: 0},
        scratch_shapes=[
            pltpu.VMEM((size, side, side), f32),
            pltpu.SMEM((size + 1,), jnp.int32),
            pltpu.SemaphoreType.DMA((size,)),
            pltpu.SemaphoreType.DMA((size,)),
        ],
        compiler_params=pltpu.CompilerParams(vmem_limit_bytes=VMEM_LIMIT),
        name="place",
    )(labels, owner, tiles, front)


def bdot(a, b, dims):
    return lax.dot_general(a, b, (dims, ((), ())), precision=highest, preferred_element_type=f32)


STEP = 4


def eliminate(block):
    side = block.shape[0]
    lanes = lax.broadcasted_iota(jnp.int32, (1, side), 1)
    left = block
    right = jnp.where(
        lax.broadcasted_iota(jnp.int32, (side, side), 0) == lax.broadcasted_iota(jnp.int32, (side, side), 1), 1.0, 0.0
    )
    upper_rows, inverse_rows = [], []
    for k in range(0, side, STEP):
        base = k // 8 * 8
        cut = base - (side - left.shape[0])
        left, right = left[cut:], right[cut:]
        height = left.shape[0]
        wide = [jnp.broadcast_to(left[:, k + i : k + i + 1], (height, side)) for i in range(STEP)]
        cols, ups, invs = [], [], []
        for i in range(STEP):
            at = k + i - base
            col, up, inv = wide[i], left[at : at + 1], right[at : at + 1]
            for j in range(i):
                factor = cols[j][at : at + 1]
                col = col - cols[j] * factor
                up = up - ups[j] * factor
                inv = inv - invs[j] * factor
            scale = lax.rsqrt(col[at : at + 1])
            cols.append(col * scale)
            ups.append(up * scale)
            invs.append(inv * scale)
            upper_rows.append(jnp.where(lanes >= k + i, ups[i], 0.0))
            inverse_rows.append(invs[i])
        for i in range(STEP):
            left = left - cols[i] * ups[i]
            right = right - cols[i] * invs[i]
    return jnp.concatenate(upper_rows, axis=0), jnp.concatenate(inverse_rows, axis=0)


def decode_block(coded, lead):
    head = coded[lead:].astype(jnp.int32).astype(f32)[:, :lead]
    block = coded[:lead, :lead].astype(jnp.int32).astype(f32) * jnp.exp2(head[0:1])
    diagonal = (head[2:3] + head[3:4] * (1.0 / 32768.0)) * jnp.exp2(head[1:2])
    on = lax.broadcasted_iota(jnp.int32, block.shape, 0) == lax.broadcasted_iota(jnp.int32, block.shape, 1)
    return jnp.where(on, diagonal, block)


def factor(first, block, columns_ref, panel_ref, weights_ref):
    rows, lead = columns_ref.shape
    side = lead // 2
    eye = lax.broadcasted_iota(jnp.int32, (side, side), 0) == lax.broadcasted_iota(jnp.int32, (side, side), 1)
    b11, b21t, b22 = block[:side, :side], block[:side, side:], block[side:, side:]
    nt, nn = ((1,), (1,)), ((1,), (0,))
    up_one, inv_one = eliminate((b11 + b11.T) * 0.5)
    below = bdot(b21t.T, inv_one, nt)
    up_two, inv_two = eliminate((b22 + b22.T) * 0.5 - bdot(below, below, nt))
    corner = -bdot(inv_two, bdot(below, inv_one, nn), nn)
    left, right = columns_ref[:, :side], columns_ref[:, side:]
    panel_left = bdot(left, inv_one, nt)
    panel_right = bdot(left, corner, nt) + bdot(right, inv_two, nt)
    weight_left = bdot(panel_left, inv_one, nn) + bdot(panel_right, corner, nn)
    weight_right = bdot(panel_right, inv_two, nn)

    def put(low, cols, panel, weight):
        high = low + panel.shape[0]
        panel_ref[low:high, cols] = panel
        hi = weight.astype(bf16)
        weights_ref[low:high, cols] = hi
        weights_ref[rows + low : rows + high, cols] = (weight - hi.astype(f32)).astype(bf16)

    before, after = slice(0, side), slice(side, lead)
    put(0, before, panel_left, weight_left)
    put(0, after, panel_right, weight_right)

    @pl.when(first == 0)
    def _():
        one_eye, zero = jnp.where(eye, 1.0, 0.0), jnp.zeros((side, side), f32)
        put(0, before, up_one.T, one_eye)
        put(0, after, zero, zero)
        put(side, before, below, zero)
        put(side, after, up_two.T, one_eye)


def front_kernel(tile_rows, slots, starts, info_ref, labels_ref, columns_ref, tiles_ref, front_ref, *refs):
    count = len(starts) - 1
    parts, out_ref = refs[:count], refs[count]
    held, coded, weights, panel, in_sems, part_sems, out_sems = refs[count + 1 :]
    rows, lead = columns_ref.shape
    side = tiles_ref.shape[2]
    steps = starts[-1]
    part_copies = [
        pltpu.make_async_copy(part, coded.at[pl.ds(low, high - low)], part_sems.at[i])
        for i, (part, low, high) in enumerate(zip(parts, starts, starts[1:]))
    ]
    columns_of = lambda g: pl.ds(pl.multiple_of(g * rows, rows), rows)
    in_copies = [
        pltpu.make_async_copy(front_ref.at[:, columns_of(g)], held.at[:, columns_of(g)], in_sems.at[g])
        for g in range(steps)
    ]
    for copy in part_copies + in_copies:
        copy.start()
    for copy in part_copies:
        copy.wait()
    factor(info_ref[0], decode_block(coded[info_ref[1]], lead), columns_ref, panel, weights)
    for copy in in_copies:
        copy.wait()

    def add(n):
        d, s = n // FIRST, n % FIRST
        label = labels_ref[d * slots + s]
        q, col = label // tile_rows, label % tile_rows

        @pl.when((label >= 0) & (col >= 2))
        def _():
            at = (pl.ds(pl.multiple_of(q * side, side), side),
                  pl.ds(pl.multiple_of(col * side, side), side))
            held[at] = held[at] + tiles_ref[d, pl.ds(pl.multiple_of(s * side, side), side)].astype(f32)

    loop(tiles_ref.shape[0] * FIRST, add)
    dot = functools.partial(jnp.dot, preferred_element_type=f32)

    def out_copy(g):
        at = columns_of(info_ref[2 + g])
        return pltpu.make_async_copy(held.at[:, at], out_ref.at[:, at], out_sems.at[g])

    def step(g):
        block = info_ref[2 + g]
        values = coded[g, :lead].astype(jnp.int32)
        scale = jnp.exp2(coded[g, lead:].astype(jnp.int32).astype(f32)[0:1])
        lower = ((values + 128) & 255) - 128
        hi = (values - lower).astype(f32).astype(bf16)
        lo = lower.astype(f32).astype(bf16)
        both = dot(weights[...], hi)
        total = both[:rows] + both[rows:] + dot(weights[:rows], lo)
        held[:, columns_of(block)] = held[:, columns_of(block)] - total * scale

        @pl.when(block == 0)
        def _():
            held[:, :lead] = panel[...]

        out_copy(g).start()

    loop(steps, step)
    loop(steps, lambda g: out_copy(g).wait())


def make_front(info, labels, columns, arrived, frontal, parts, tile_rows):
    rows, order = frontal.shape
    lead = columns.shape[1]
    starts = [0]
    for part in parts:
        starts.append(starts[-1] + part.shape[0])
    smem, anyw = (pl.BlockSpec(memory_space=m) for m in (pltpu.SMEM, pl.ANY))
    return pl.pallas_call(
        functools.partial(front_kernel, tile_rows, labels.shape[1], tuple(starts)),
        grid=(1,),
        out_shape=jax.ShapeDtypeStruct((rows, order), f32),
        in_specs=[
            smem, smem,
            pl.BlockSpec((rows, lead), lambda i: (0, 0)),
            pl.BlockSpec(arrived.shape, lambda i: (0, 0, 0)),
            anyw,
        ] + [anyw] * len(parts),
        out_specs=anyw,
        scratch_shapes=[
            pltpu.VMEM((rows, order), f32),
            pltpu.VMEM((starts[-1], lead + HEAD, rows), jnp.int16),
            pltpu.VMEM((2 * rows, lead), bf16),
            pltpu.VMEM((rows, lead), f32),
            pltpu.SemaphoreType.DMA((starts[-1],)),
            pltpu.SemaphoreType.DMA((len(parts),)),
            pltpu.SemaphoreType.DMA((starts[-1],)),
        ],
        compiler_params=pltpu.CompilerParams(vmem_limit_bytes=VMEM_LIMIT),
        cost_estimate=pl.CostEstimate(
            flops=6 * rows * order * lead, bytes_accessed=8 * rows * order, transcendentals=0
        ),
        name="front",
    )(info, labels.reshape(-1), columns, arrived, frontal, *parts)


def local_fast(frontal, child_tiles, child_rows, child_cols):
    rows, order = frontal.shape
    side = child_tiles.shape[1]
    lead = 2 * side
    tile_rows = order // side
    devices = lax.axis_size("row")
    layers = devices // 4
    slots = MOST_SAME * rows // side
    row = lax.axis_index("row").astype(jnp.int32)
    every = [(z, x, c) for z in range(layers) for x in range(2) for c in range(2)]
    index = lambda z, x, c: z % layers * 4 + x * 2 + c
    over_core = [(index(z, x, c), index(z, x, 1 - c)) for z, x, c in every]
    over_x = [(index(z, x, c), index(z, 1 - x, c)) for z, x, c in every]
    over_z = lambda s: [(index(z, x, c), index(z + s, x, c)) for z, x, c in every]
    send = lambda x, pairs: lax.ppermute(x, "row", pairs)
    exchange = lambda x: lax.all_to_all(x, "row", split_axis=0, concat_axis=0, tiled=True)

    first, second, third = pack(child_tiles, child_rows, child_cols, devices, tile_rows)
    one = exchange(first)
    head = one[:, FIRST * side : FIRST * side + 2, :slots].astype(f32)
    labels = head[:, 0].astype(jnp.int32) - 1
    columns, narrow = lead_columns(row[None], labels, frontal, one, tile_rows)

    join = lambda *x: jnp.concatenate(x, axis=0)
    tie = lax.optimization_barrier
    narrow, second = tie((narrow, second))
    up, down, over = send(narrow, over_z(1)), send(narrow, over_z(layers - 1)), send(narrow, over_x)
    narrow, up, down, over = tie((narrow, up, down, over))
    near, beside = join(narrow, over), join(up, down)
    far = [send(narrow, over_z(s)) for s in range(2, layers - 1)]
    beside_x, near_c = send(beside, over_x), send(near, over_core)
    far, beside_x, near_c, near, beside = tie((far, beside_x, near_c, near, beside))
    far, beside = join(*far), join(beside, beside_x)
    far_x, beside_c = send(far, over_x), send(beside, over_core)
    far_x, beside_c, far = tie((far_x, beside_c, far))
    far = join(far, far_x)
    far_c = send(far, over_core)
    far_c, second = tie((far_c, second))
    two = exchange(second)
    parts = [near, near_c, beside, beside_c, far, far_c]

    z, x, c = row // 4, row // 2 % 2, row % 2
    cols = []
    for offsets in ([0], [1, layers - 1], list(range(2, layers - 1))):
        cols += [
            (z - dz) % layers * 4 + (x ^ dx) * 2 + (c ^ dc) for dc in range(2) for dx in range(2) for dz in offsets
        ]
    at = sum(jnp.where(col == 0, g, 0) for g, col in enumerate(cols))
    info = jnp.stack([row, at] + cols).astype(jnp.int32)
    front = make_front(info, labels, columns, one, frontal, parts, tile_rows)

    wanted = jnp.where(labels % tile_rows < 2, -1, labels)
    front, two = tie((front, two))
    front = place(front, wanted[:, FIRST : FIRST + SECOND], two, tile_rows)
    flags = jnp.max(head[:, 1, :2], axis=0)
    flags = jnp.maximum(flags, lax.ppermute(flags, "groups", [(0, 1), (1, 0)]))
    front, third, labels = tie((front, third, wanted[:, FIRST + SECOND :]))
    case = jnp.where(flags[0] > 0, 2, jnp.where(flags[1] > 0, 1, 0)).astype(jnp.int32)

    def spread(x, axis):
        every = exchange(jnp.broadcast_to(x[None], (devices,) + x.shape))
        return every.reshape(order, x.shape[1])

    return lax.switch(
        case,
        [
            lambda front, third, labels, *args: front,
            lambda front, third, labels, *args: place(front, labels, exchange(third), tile_rows),
            lambda front, third, labels, *args: local_small(*args, spread),
        ],
        front, third, labels, frontal, child_tiles, child_rows, child_cols,
    )


def gather_rows(x, axis):
    return lax.all_gather(x, axis, axis=0, tiled=True)


def factor_rows(column_block, square_block, low_edge):
    tile_side = square_block.shape[0]
    factor = jnp.linalg.cholesky(square_block)
    identity = jnp.eye(tile_side, dtype=column_block.dtype)
    inverse = jax.scipy.linalg.solve_triangular(factor, identity, lower=True)
    solved = jnp.dot(column_block, inverse.T, precision=highest)
    row_ids = jnp.arange(column_block.shape[0], dtype=jnp.int32)
    inside = (row_ids >= low_edge) & (row_ids < low_edge + tile_side)
    within = jnp.take(factor, jnp.clip(row_ids - low_edge, 0, tile_side - 1), axis=0)
    before = row_ids < low_edge
    return jnp.where(
        inside[:, None], within, jnp.where(before[:, None], jnp.zeros_like(solved), solved)
    )


def apply_panel(current, panel_rows, update, low_edge):
    tile_side = panel_rows.shape[1]
    col_ids = jnp.arange(current.shape[1], dtype=jnp.int32)[None, :]
    current = jnp.where(col_ids >= low_edge + tile_side, current - update, current)
    return current.at[:, low_edge : low_edge + tile_side].set(panel_rows)


def pack_pieces(child_tiles, child_rows, child_cols, selected, rows_dev, order):
    tile_total = child_tiles.shape[0]
    tile_side = child_tiles.shape[1]
    tile_rows = order // tile_side
    piece_rows = min(rows_dev, tile_side)
    per_tile = tile_side // piece_rows
    capacity = MOST_SAME * max(1, rows_dev // tile_side)
    devices = lax.axis_size("row")
    parent = child_rows[:, 0]
    grouping = parent * tile_side // max(rows_dev, tile_side)
    sequence = jnp.arange(tile_total, dtype=jnp.int32)
    earlier = (
        (grouping[:, None] == grouping[None, :])
        & (sequence[None, :] < sequence[:, None])
        & selected[None, :]
    )
    slot_ids = jnp.sum(earlier.astype(jnp.int32), axis=1)
    offsets = (
        parent[:, None] * tile_side + jnp.arange(per_tile, dtype=jnp.int32)[None, :] * piece_rows
    )
    targets = jnp.where(selected[:, None], offsets // rows_dev, devices)
    local_ids = offsets % rows_dev // piece_rows
    slot_grid = jnp.broadcast_to(slot_ids[:, None], targets.shape)
    pieces = child_tiles.reshape(tile_total, per_tile, piece_rows, tile_side)
    outgoing = (
        jnp.zeros((devices, capacity, piece_rows, tile_side), child_tiles.dtype)
        .at[targets, slot_grid]
        .set(pieces, mode="drop")
    )
    position = local_ids * tile_rows + child_cols[:, None]
    labels = (
        jnp.full((devices, capacity), -1, jnp.int32)
        .at[targets, slot_grid]
        .set(position, mode="drop")
    )
    return (outgoing, labels)


def place_pieces(arrived, arrived_ids, rows_dev, order):
    piece_rows = arrived.shape[2]
    tile_side = arrived.shape[3]
    tile_rows = order // tile_side
    blocks_dev = rows_dev // piece_rows
    count = arrived.shape[0] * arrived.shape[1]
    selector = (
        arrived_ids.reshape(-1, 1) == jnp.arange(blocks_dev * tile_rows, dtype=jnp.int32)[None, :]
    ).astype(arrived.dtype)
    selector = selector.reshape(count, blocks_dev, tile_rows)
    flattened = arrived.reshape(count, piece_rows, tile_side)
    assembled_part = jnp.einsum(
        "nqc,nsw->qscw", selector, flattened, preferred_element_type=jnp.float32
    )
    return assembled_part.reshape(rows_dev, order)


def local_small(frontal, child_tiles, child_rows, child_cols, gather):
    rows_dev = frontal.shape[0]
    order = frontal.shape[1]
    tile_side = child_tiles.shape[1]
    first_row = lax.axis_index("row") * rows_dev
    current = frontal
    everything = jnp.ones(child_cols.shape, dtype=bool)
    outgoing, labels = pack_pieces(child_tiles, child_rows, child_cols, everything, rows_dev, order)
    arrived, arrived_ids = (
        lax.all_to_all(outgoing, "row", split_axis=0, concat_axis=0, tiled=True),
        lax.all_to_all(labels, "row", split_axis=0, concat_axis=0, tiled=True),
    )
    current = current + place_pieces(arrived, arrived_ids, rows_dev, order)
    leading = gather(current[:, : 2 * tile_side], "row")
    first_all = factor_rows(leading[:, :tile_side], leading[:tile_side, :tile_side], 0)
    second_block = leading[:, tile_side:] - jnp.dot(
        first_all, first_all[tile_side : 2 * tile_side].T, precision=highest
    )
    second_all = factor_rows(second_block, second_block[tile_side : 2 * tile_side], tile_side)
    for panel_index, panel_all in enumerate((first_all, second_all)):
        low_edge = panel_index * tile_side
        panel_own = lax.dynamic_slice_in_dim(panel_all, first_row, rows_dev, 0)
        update = jnp.dot(panel_own, panel_all.T, precision=highest)
        current = apply_panel(current, panel_own, update, low_edge)
    return current


def local(frontal, child_tiles, child_rows, child_cols):
    rows, order = frontal.shape
    side = child_tiles.shape[1]
    devices = lax.axis_size("row")
    wide = rows >= 2 * side and rows % side == 0 and MOST_SAME * rows // side > FIRST + SECOND
    if wide and order == devices * rows and devices % 4 == 0 and devices >= 16 and lax.axis_size("groups") == 2:
        return local_fast(frontal, child_tiles, child_rows, child_cols)
    return local_small(frontal, child_tiles, child_rows, child_cols, gather_rows)


def solution(mesh):
    return jax.shard_map(
        local,
        mesh=mesh,
        in_specs=(
            P(("groups", "row"), None),
            P(("groups", "row"), None, None),
            P(("groups", "row"), None),
            P(("groups", "row")),
        ),
        out_specs=P(("groups", "row"), None),
        check_vma=False,
    )
```

profile of v0, /device:TPU:0, one launch (start us, length us, event | category | flops | bytes accessed | tf_op | source)
XLA Modules:
  0.0 153.8 jit_solution(7357823995831374368)
XLA Ops:
  0.0 5.9 %pack.1 = (bf16[16,400,128]{2,1,0:T(8,128)(2,1)}, bf16[16,384,128]{2,1,0:T(8,128)(2,1)}, bf16[16,256,128]{2,1,0:T(8,128)(2,1)}) custom-call(s32[64]{0:T(128)} %bitcast.103, s32[64]{0:T(128)} %cols_ref.1, bf16[64,128,128]{2,1,0:T(8,128)(2,1)} %tiles_ref.1), custom_call_target="tpu_custom_call" | custom-call | tf_op jit(solution)/shard_map/pack/pallas_call | solution.py:95
  5.9 7.4 %all-to-all-start.4 = ((bf16[16,400,128]{2,1,0:T(8,128)(2,1)}), bf16[16,400,128]{2,1,0:T(8,128)(2,1)S(1)}, u32[]{:S(2)}, u32[]{:S(2)}) async-start(bf16[16,400,128]{2,1,0:T(8,128)(2,1)} %get-tuple-element.84), calls=%async_computation.4 | async-start | bytes 3276800 | tf_op jit(solution)/shard_map/all_to_all | solution.py:454
  13.3 33.1 %all-to-all-done.4.tiles_ref = bf16[16,400,128]{2,1,0:T(8,128)(2,1)S(1)} async-done(((bf16[16,400,128]{2,1,0:T(8,128)(2,1)}), bf16[16,400,128]{2,1,0:T(8,128)(2,1)S(1)}, u32[]{:S(2)}, u32[]{:S(2)}) %all-to-all-start.4) | async-done | bytes 1638432 | tf_op jit(solution)/shard_map/all_to_all | solution.py:454
  46.4 0.0 copy-start.6
  46.5 0.7 sub.68.labels_ref
  47.2 0.4 copy-done.6
  47.6 4.2 %lead_columns.1 = (f32[512,256]{1,0:T(8,128)}, s16[1,272,512]{2,1,0:T(8,128)(2,1)}) custom-call(s32[1]{0:T(128)} %bitcast.23.row_ref, s32[128]{0:T(128)} %sub.68.labels_ref, f32[512,8192]{1,0:T(8,128)} %front_ref.3, bf16[16,400,128]{2,1,0:T(8,128)(2,1)} %copy-done.6), custom_call_target="tpu_custom_call" | custom-call | tf_op jit(solution)/shard_map/lead_columns/pallas_call | solution.py:161
  51.8 4.9 %collective-permute-start.1 = (s16[1,272,512]{2,1,0:T(8,128)(2,1)}, s16[1,272,512]{2,1,0:T(8,128)(2,1)S(1)}, u32[]{:S(2)}, u32[]{:S(2)}) collective-permute-start(s16[1,272,512]{2,1,0:T(8,128)(2,1)} %get-tuple-element.89), channel_id=1, source_target_pairs={{0,4},{1,5},{2,6},{3,7},{4,8},{5,9},{6,10},{7,11},{8,12},{9,13},{1... | collective-permute-start | bytes 835592 | tf_op jit(solution)/shard_map/ppermute | solution.py:453
  56.7 0.0 collective-permute-start.2
  56.7 3.6 %collective-permute-start.3 = (s16[1,272,512]{2,1,0:T(8,128)(2,1)}, s16[1,272,512]{2,1,0:T(8,128)(2,1)S(1)}, u32[]{:S(2)}, u32[]{:S(2)}) collective-permute-start(s16[1,272,512]{2,1,0:T(8,128)(2,1)} %get-tuple-element.89), channel_id=1, source_target_pairs={{0,2},{1,3},{2,0},{3,1},{4,6},{5,7},{6,4},{7,5},{8,10},{9,11},{10,... | collective-permute-start | bytes 835592 | tf_op jit(solution)/shard_map/ppermute | solution.py:453
  60.3 4.2 %collective-permute-done.1 = s16[1,272,512]{2,1,0:T(8,128)(2,1)S(1)} collective-permute-done((s16[1,272,512]{2,1,0:T(8,128)(2,1)}, s16[1,272,512]{2,1,0:T(8,128)(2,1)S(1)}, u32[]{:S(2)}, u32[]{:S(2)}) %collective-permute-start.1) | collective-permute-done | bytes 278560 | tf_op jit(solution)/shard_map/ppermute | solution.py:453
  64.5 5.9 %collective-permute-done.2 = s16[1,272,512]{2,1,0:T(8,128)(2,1)S(1)} collective-permute-done((s16[1,272,512]{2,1,0:T(8,128)(2,1)}, s16[1,272,512]{2,1,0:T(8,128)(2,1)S(1)}, u32[]{:S(2)}, u32[]{:S(2)}) %collective-permute-start.2) | collective-permute-done | bytes 278560 | tf_op jit(solution)/shard_map/ppermute | solution.py:453
  70.4 0.0 collective-permute-done.3
  70.4 1.0 constant_dynamic-update-slice_fusion.3
  71.4 0.0 copy-start.11
  71.4 0.1 collective-permute-start.6
  71.5 3.3 %collective-permute-start.5 = (s16[2,272,512]{2,1,0:T(8,128)(2,1)S(1)}, s16[2,272,512]{2,1,0:T(8,128)(2,1)S(1)}, u32[]{:S(2)}, u32[]{:S(2)}) collective-permute-start(s16[2,272,512]{2,1,0:T(8,128)(2,1)S(1)} %constant_dynamic-update-slice_fusion), channel_id=1, source_target_pairs={{0,2},{1,3},{2,0},{3,1},{4,6},{5,7},{6,4},{7,5},{8,10},{9,11},{10,... | collective-permute-start | bytes 1671176 | tf_op jit(solution)/shard_map/ppermute | solution.py:453
  74.9 0.6 collective-permute-start.4
  75.5 15.3 %collective-permute-done.4 = s16[1,272,512]{2,1,0:T(8,128)(2,1)S(1)} collective-permute-done((s16[1,272,512]{2,1,0:T(8,128)(2,1)}, s16[1,272,512]{2,1,0:T(8,128)(2,1)S(1)}, u32[]{:S(2)}, u32[]{:S(2)}) %collective-permute-start.4) | collective-permute-done | bytes 278560 | tf_op jit(solution)/shard_map/ppermute | solution.py:453
  90.7 0.0 collective-permute-done.6.refs_1_
  90.7 0.0 copy-start.13
  90.7 0.9 copy-done.13
  91.6 0.0 collective-permute-done.5
  91.7 0.0 copy-start.9
  91.7 0.1 collective-permute-start.8
  91.8 0.4 collective-permute-start.7
  92.2 8.6 %collective-permute-done.7 = s16[1,272,512]{2,1,0:T(8,128)(2,1)S(1)} collective-permute-done((s16[1,272,512]{2,1,0:T(8,128)(2,1)S(1)}, s16[1,272,512]{2,1,0:T(8,128)(2,1)S(1)}, u32[]{:S(2)}, u32[]{:S(2)}) %collective-permute-start.7) | collective-permute-done | bytes 278560 | tf_op jit(solution)/shard_map/ppermute | solution.py:453
  100.8 0.0 collective-permute-done.8.refs_3_
  100.8 0.0 copy-start.12
  100.9 0.0 copy-start.10
  100.9 0.1 collective-permute-start.9
  101.0 2.1 %collective-permute-done.9.refs_5_ = s16[2,272,512]{2,1,0:T(8,128)(2,1)} collective-permute-done((s16[2,272,512]{2,1,0:T(8,128)(2,1)S(1)}, s16[2,272,512]{2,1,0:T(8,128)(2,1)}, u32[]{:S(2)}, u32[]{:S(2)}) %collective-permute-start.9) | collective-permute-done | bytes 557088 | tf_op jit(solution)/shard_map/ppermute | solution.py:453
  103.1 4.4 %all-to-all-start.5 = ((bf16[16,384,128]{2,1,0:T(8,128)(2,1)}), bf16[16,384,128]{2,1,0:T(8,128)(2,1)}, u32[]{:S(2)}, u32[]{:S(2)}) async-start(bf16[16,384,128]{2,1,0:T(8,128)(2,1)} %get-tuple-element.103), calls=%async_computation.5 | async-start | bytes 3145728 | tf_op jit(solution)/shard_map/all_to_all | solution.py:454
  107.7 0.6 stack.75.info_ref
  108.3 0.1 copy.48
  108.4 0.1 copy.49
  108.5 0.1 reshape.192.labels_ref
  108.6 0.0 copy-start.14
  108.6 1.6 %collective-permute-start = (f32[2]{0:T(128)S(1)}, f32[2]{0:T(128)S(1)}, u32[]{:S(2)}, u32[]{:S(2)}) collective-permute-start(f32[2]{0:T(128)S(1)} %slice_reduce_fusion), channel_id=1, source_target_pairs={{0,16},{16,0},{1,17},{17,1},{2,18},{18,2},{3,19},{19,3},{4,20},{20... | collective-permute-start | bytes 32 | tf_op jit(solution)/shard_map/ppermute | solution.py:494
  110.2 0.2 select_reduce_fusion.3
  110.4 0.6 compare_select_fusion.14.owner_ref
  110.9 1.3 collective-permute-done
  112.2 0.6 fusion.42
  114.1 0.0 copy-done.11
  114.1 0.0 copy-done.9
  114.2 0.0 copy-done.12
  114.2 0.0 copy-done.10
  114.2 33.7 %front.1.front_ref = f32[512,8192]{1,0:T(8,128)} custom-call(s32[18]{0:T(128)} %stack.75.info_ref, s32[128]{0:T(128)} %sub.68.labels_ref, f32[512,256]{1,0:T(8,128)} %get-tuple-element.85.columns_ref, bf16[16,400,128]{2,1,0:T(8,128)(2,1)} %copy-done.6, f32[512,8192]{1,0:T(8,128)} %front_ref.3, s16[2,272,512]{2,1,0:T(8,128)(2,1)} %copy-done.11, ...), custom_call_target="tpu_custom_call" | custom-call | flops 6442450944 | bytes 33554432 | tf_op jit(solution)/shard_map/front/pallas_call | solution.py:411
  147.9 0.0 copy-done.14
  147.9 0.0 copy-start.7
  147.9 0.0 copy-start.16
  147.9 0.0 copy-start.17
  147.9 0.0 all-to-all-done.5.tiles_ref
  148.0 5.4 %place.3 = f32[512,8192]{1,0:T(8,128)} custom-call(s32[48]{0:T(128)} %copy-done.14, s32[48]{0:T(128)} %compare_select_fusion.14.owner_ref, bf16[16,384,128]{2,1,0:T(8,128)(2,1)} %all-to-all-done.5.tiles_ref, f32[512,8192]{1,0:T(8,128)} %front.1.front_ref), custom_call_target="tpu_custom_call", output_to_operand_aliasing={{}: (3, {})} | custom-call | tf_op jit(solution)/shard_map/place/pallas_call | solution.py:237
  153.4 0.0 copy-done.7
  153.4 0.0 copy-done.16
  153.4 0.0 copy-done.17
  153.4 0.2 conditional.1
  (14 shorter events, 0.3 us)
Async XLA Ops:
  5.9 40.5 %all-to-all-start.4 = ((bf16[16,400,128]{2,1,0:T(8,128)(2,1)}), bf16[16,400,128]{2,1,0:T(8,128)(2,1)S(1)}, u32[]{:S(2)}, u32[]{:S(2)}) async-start(bf16[16,400,128]{2,1,0:T(8,128)(2,1)} %get-tuple-element.84), calls=%async_computation.4 | async-start | bytes 3276800 | tf_op jit(solution)/shard_map/all_to_all | solution.py:454
  46.4 1.2 copy-start.6
  51.8 12.7 %collective-permute-start.1 = (s16[1,272,512]{2,1,0:T(8,128)(2,1)}, s16[1,272,512]{2,1,0:T(8,128)(2,1)S(1)}, u32[]{:S(2)}, u32[]{:S(2)}) collective-permute-start(s16[1,272,512]{2,1,0:T(8,128)(2,1)} %get-tuple-element.89), channel_id=1, source_target_pairs={{0,4},{1,5},{2,6},{3,7},{4,8},{5,9},{6,10},{7,11},{8,12},{9,13},{1... | collective-permute-start | bytes 835592 | tf_op jit(solution)/shard_map/ppermute | solution.py:453
  56.7 13.7 %collective-permute-start.2 = (s16[1,272,512]{2,1,0:T(8,128)(2,1)}, s16[1,272,512]{2,1,0:T(8,128)(2,1)S(1)}, u32[]{:S(2)}, u32[]{:S(2)}) collective-permute-start(s16[1,272,512]{2,1,0:T(8,128)(2,1)} %get-tuple-element.89), channel_id=1, source_target_pairs={{0,12},{1,13},{2,14},{3,15},{4,0},{5,1},{6,2},{7,3},{8,4},{9,5},{1... | collective-permute-start | bytes 835592 | tf_op jit(solution)/shard_map/ppermute | solution.py:453
  56.7 13.7 %collective-permute-start.3 = (s16[1,272,512]{2,1,0:T(8,128)(2,1)}, s16[1,272,512]{2,1,0:T(8,128)(2,1)S(1)}, u32[]{:S(2)}, u32[]{:S(2)}) collective-permute-start(s16[1,272,512]{2,1,0:T(8,128)(2,1)} %get-tuple-element.89), channel_id=1, source_target_pairs={{0,2},{1,3},{2,0},{3,1},{4,6},{5,7},{6,4},{7,5},{8,10},{9,11},{10,... | collective-permute-start | bytes 835592 | tf_op jit(solution)/shard_map/ppermute | solution.py:453
  71.4 42.8 %copy-start.11 = (s16[2,272,512]{2,1,0:T(8,128)(2,1)}, s16[2,272,512]{2,1,0:T(8,128)(2,1)S(1)}, u32[]{:S(2)}) copy-start(s16[2,272,512]{2,1,0:T(8,128)(2,1)S(1)} %constant_dynamic-update-slice_fusion.2.refs_0_) | copy-start | bytes 1671172
  71.4 19.3 %collective-permute-start.6 = (s16[2,272,512]{2,1,0:T(8,128)(2,1)S(1)}, s16[2,272,512]{2,1,0:T(8,128)(2,1)S(1)}, u32[]{:S(2)}, u32[]{:S(2)}) collective-permute-start(s16[2,272,512]{2,1,0:T(8,128)(2,1)S(1)} %constant_dynamic-update-slice_fusion.2.refs_0_), channel_id=1, source_target_pairs={{0,1},{1,0},{2,3},{3,2},{4,5},{5,4},{6,7},{7,6},{8,9},{9,8},{10,11... | collective-permute-start | bytes 1671176 | tf_op jit(solution)/shard_map/ppermute | solution.py:453
  71.5 20.1 %collective-permute-start.5 = (s16[2,272,512]{2,1,0:T(8,128)(2,1)S(1)}, s16[2,272,512]{2,1,0:T(8,128)(2,1)S(1)}, u32[]{:S(2)}, u32[]{:S(2)}) collective-permute-start(s16[2,272,512]{2,1,0:T(8,128)(2,1)S(1)} %constant_dynamic-update-slice_fusion), channel_id=1, source_target_pairs={{0,2},{1,3},{2,0},{3,1},{4,6},{5,7},{6,4},{7,5},{8,10},{9,11},{10,... | collective-permute-start | bytes 1671176 | tf_op jit(solution)/shard_map/ppermute | solution.py:453
  74.9 15.9 %collective-permute-start.4 = (s16[1,272,512]{2,1,0:T(8,128)(2,1)}, s16[1,272,512]{2,1,0:T(8,128)(2,1)S(1)}, u32[]{:S(2)}, u32[]{:S(2)}) collective-permute-start(s16[1,272,512]{2,1,0:T(8,128)(2,1)} %get-tuple-element.89), channel_id=1, source_target_pairs={{0,8},{1,9},{2,10},{3,11},{4,12},{5,13},{6,14},{7,15},{8,0},{9,1},... | collective-permute-start | bytes 835592 | tf_op jit(solution)/shard_map/ppermute | solution.py:453
  90.7 0.9 copy-start.13
  91.7 22.5 %copy-start.9 = (s16[4,272,512]{2,1,0:T(8,128)(2,1)}, s16[4,272,512]{2,1,0:T(8,128)(2,1)S(1)}, u32[]{:S(2)}) copy-start(s16[4,272,512]{2,1,0:T(8,128)(2,1)S(1)} %constant_dynamic-update-slice_fusion.4.refs_2_) | copy-start | bytes 3342340
  91.7 9.2 %collective-permute-start.8 = (s16[4,272,512]{2,1,0:T(8,128)(2,1)S(1)}, s16[4,272,512]{2,1,0:T(8,128)(2,1)S(1)}, u32[]{:S(2)}, u32[]{:S(2)}) collective-permute-start(s16[4,272,512]{2,1,0:T(8,128)(2,1)S(1)} %constant_dynamic-update-slice_fusion.4.refs_2_), channel_id=1, source_target_pairs={{0,1},{1,0},{2,3},{3,2},{4,5},{5,4},{6,7},{7,6},{8,9},{9,8},{10,11... | collective-permute-start | bytes 3342344 | tf_op jit(solution)/shard_map/ppermute | solution.py:453
  91.8 9.1 %collective-permute-start.7 = (s16[1,272,512]{2,1,0:T(8,128)(2,1)S(1)}, s16[1,272,512]{2,1,0:T(8,128)(2,1)S(1)}, u32[]{:S(2)}, u32[]{:S(2)}) collective-permute-start(s16[1,272,512]{2,1,0:T(8,128)(2,1)S(1)} %collective-permute-done.4), channel_id=1, source_target_pairs={{0,2},{1,3},{2,0},{3,1},{4,6},{5,7},{6,4},{7,5},{8,10},{9,11},{10,... | collective-permute-start | bytes 835592 | tf_op jit(solution)/shard_map/ppermute | solution.py:453
  100.8 13.3 %copy-start.12 = (s16[4,272,512]{2,1,0:T(8,128)(2,1)}, s16[4,272,512]{2,1,0:T(8,128)(2,1)S(1)}, u32[]{:S(2)}) copy-start(s16[4,272,512]{2,1,0:T(8,128)(2,1)S(1)} %collective-permute-done.8.refs_3_) | copy-start | bytes 3342340
  100.9 13.3 %copy-start.10 = (s16[2,272,512]{2,1,0:T(8,128)(2,1)}, s16[2,272,512]{2,1,0:T(8,128)(2,1)S(1)}, u32[]{:S(2)}) copy-start(s16[2,272,512]{2,1,0:T(8,128)(2,1)S(1)} %constant_dynamic-update-slice_fusion.6.refs_4_) | copy-start | bytes 1671172
  100.9 2.2 %collective-permute-start.9 = (s16[2,272,512]{2,1,0:T(8,128)(2,1)S(1)}, s16[2,272,512]{2,1,0:T(8,128)(2,1)}, u32[]{:S(2)}, u32[]{:S(2)}) collective-permute-start(s16[2,272,512]{2,1,0:T(8,128)(2,1)S(1)} %constant_dynamic-update-slice_fusion.6.refs_4_), channel_id=1, source_target_pairs={{0,1},{1,0},{2,3},{3,2},{4,5},{5,4},{6,7},{7,6},{8,9},{9,8},{10,11... | collective-permute-start | bytes 1671176 | tf_op jit(solution)/shard_map/ppermute | solution.py:453
  103.1 44.9 %all-to-all-start.5 = ((bf16[16,384,128]{2,1,0:T(8,128)(2,1)}), bf16[16,384,128]{2,1,0:T(8,128)(2,1)}, u32[]{:S(2)}, u32[]{:S(2)}) async-start(bf16[16,384,128]{2,1,0:T(8,128)(2,1)} %get-tuple-element.103), calls=%async_computation.5 | async-start | bytes 3145728 | tf_op jit(solution)/shard_map/all_to_all | solution.py:454
  108.6 39.3 %copy-start.14 = (s32[48]{0:T(128)}, s32[48]{0:T(128)S(1)}, u32[]{:S(2)}) copy-start(s32[48]{0:T(128)S(1)} %reshape.192.labels_ref) | copy-start | bytes 580
  108.6 3.6 %collective-permute-start = (f32[2]{0:T(128)S(1)}, f32[2]{0:T(128)S(1)}, u32[]{:S(2)}, u32[]{:S(2)}) collective-permute-start(f32[2]{0:T(128)S(1)} %slice_reduce_fusion), channel_id=1, source_target_pairs={{0,16},{16,0},{1,17},{17,1},{2,18},{18,2},{3,19},{19,3},{4,20},{20... | collective-permute-start | bytes 32 | tf_op jit(solution)/shard_map/ppermute | solution.py:494
  147.9 5.4 %copy-start.7 = (bf16[64,128,128]{2,1,0:T(8,128)(2,1)S(1)}, bf16[64,128,128]{2,1,0:T(8,128)(2,1)}, u32[]{:S(2)}) copy-start(bf16[64,128,128]{2,1,0:T(8,128)(2,1)} %tiles_ref.1) | copy-start | bytes 6291460
  147.9 5.4 %copy-start.16 = (s32[64,1]{0,1:T(1,128)S(1)}, s32[64,1]{0,1:T(1,128)}, u32[]{:S(2)}) copy-start(s32[64,1]{0,1:T(1,128)} %param.18) | copy-start | bytes 772
  147.9 5.4 %copy-start.17 = (s32[64]{0:T(128)S(1)}, s32[64]{0:T(128)}, u32[]{:S(2)}) copy-start(s32[64]{0:T(128)} %cols_ref.1) | copy-start | bytes 772
where the time goes:
time: 154 us
  waiting for transfers between devices  70.4 us (46%)
  Pallas kernels  49.2 us (32%)
  starting transfers between devices  26.5 us (17%)
  local copies, waits for them, and re-layouts  4.65 us (3%)
  between operations  1.97 us (1%)
    ppermute x9, waiting for transfers between devices, local_fast(): send = lambda x, pairs: lax.ppermute(x, 'row', pairs)  36 us
    pallas_call x1, Pallas kernels, make_front(): pl.pallas_call(functools.partial(front_kernel, tile_rows, labels.shape[1]...  33.7 us
    all_to_all x2, waiting for transfers between devices, local_fast(): lax.all_to_all(x, 'row', split_axis=0, concat_axis=0, tiled=True)  33.1 us
    ppermute x9, starting transfers between devices, local_fast(): send = lambda x, pairs: lax.ppermute(x, 'row', pairs)  13.1 us
    all_to_all x2, starting transfers between devices, local_fast(): lax.all_to_all(x, 'row', split_axis=0, concat_axis=0, tiled=True)  11.8 us
    pallas_call x1, Pallas kernels, pack(): pl.pallas_call(functools.partial(pack_kernel, tile_rows, per_dev), grid=(...  5.93 us
    pallas_call x1, Pallas kernels, place(): pl.pallas_call(functools.partial(place_kernel, tile_rows), grid=(1,), out...  5.39 us
    pallas_call x1, Pallas kernels, lead_columns(): pl.pallas_call(functools.partial(lead_kernel, tile_rows, labels.shape[1])...  4.16 us
  transfers between devices with their start and end apart: 12, of which 7 were waited for; matrix products, arithmetic and copies ran while one was open for 1% of the time, Pallas kernels for 22%

commit v1 on v0

--- a/solution.py
+++ b/solution.py
@@ -17,13 +17,13 @@
 f32, bf16 = jnp.float32, jnp.bfloat16
 
 
-def loop(count, body):
-    lax.fori_loop(0, count, lambda i, carry: (body(i), carry)[1], 0)
+def loop(count, body, unroll=1):
+    lax.fori_loop(0, count, lambda i, carry: (body(i), carry)[1], 0, unroll=unroll)
 
 
 def pack_kernel(
     tile_rows, per_dev, rows_ref, cols_ref, tiles_ref, first_ref, second_ref, third_ref,
-    heads, heads_out, counts, sems, head_sem,
+    heads, heads_out, counts, sem, head_sem,
 ):
     tiles, side, _ = tiles_ref.shape
     devices = first_ref.shape[0]
@@ -50,13 +50,13 @@
             @pl.when(s < FIRST)
             def _():
                 pltpu.make_async_copy(
-                    tiles_ref.at[i], first_ref.at[d, pl.ds(s * side, side)], sems.at[i]
+                    tiles_ref.at[i], first_ref.at[d, pl.ds(s * side, side)], sem
                 ).start()
 
             @pl.when((s >= FIRST) & (s < FIRST + SECOND))
             def _():
                 pltpu.make_async_copy(
-                    tiles_ref.at[i], second_ref.at[d, pl.ds((s - FIRST) * side, side)], sems.at[i]
+                    tiles_ref.at[i], second_ref.at[d, pl.ds((s - FIRST) * side, side)], sem
                 ).start()
 
             @pl.when(s >= FIRST + SECOND)
@@ -64,15 +64,15 @@
                 pltpu.make_async_copy(
                     tiles_ref.at[i],
                     third_ref.at[d, pl.ds((s - FIRST - SECOND) * side, side)],
-                    sems.at[i],
+                    sem,
                 ).start()
 
     def most():
         return lax.fori_loop(0, devices, lambda d, m: jnp.maximum(m, counts[d]), 0)
 
-    loop(tiles, lambda i: place(i, True))
+    loop(tiles, lambda i: place(i, True), 4)
     lead_over = (most() > FIRST).astype(f32)
-    loop(tiles, lambda i: place(i, False))
+    loop(tiles, lambda i: place(i, False), 4)
     over = (most() > FIRST + SECOND).astype(f32)
     flags = jnp.where(lanes == 0, lead_over, jnp.where(lanes == 1, over, 0.0))
     marked = jnp.where((subs == 1)[None], flags[None], heads[...])
@@ -80,10 +80,7 @@
     copy = pltpu.make_async_copy(heads_out, first_ref.at[:, pl.ds(FIRST * side, HEAD)], head_sem)
     copy.start()
 
-    def finish(i):
-        pltpu.make_async_copy(tiles_ref.at[i], first_ref.at[0, pl.ds(0, side)], sems.at[i]).wait()
-
-    loop(tiles, finish)
+    pltpu.make_async_copy(tiles_ref, tiles_ref, sem).wait()
     copy.wait()
 
 
@@ -106,7 +103,7 @@
             pltpu.VMEM((devices, 8, 128), f32),
             pltpu.VMEM((devices, HEAD, 128), bf16),
             pltpu.SMEM((devices,), jnp.int32),
-            pltpu.SemaphoreType.DMA((tiles,)),
+            pltpu.SemaphoreType.DMA,
             pltpu.SemaphoreType.DMA,
         ],
         compiler_params=pltpu.CompilerParams(vmem_limit_bytes=VMEM_LIMIT),
@@ -179,9 +176,13 @@
     )(row, labels.reshape(-1), frontal, arrived)
 
 
-def place_kernel(tile_rows, labels_ref, owner_ref, tiles_ref, front_ref, out_ref, held, listed, in_sems, out_sems):
+def place_kernel(
+    tile_rows, labels_ref, owner_ref, arrived_ref, front_ref, out_ref, tiles_ref, held, listed, tile_sem, in_sems, out_sems
+):
     side = tiles_ref.shape[2]
     slots = tiles_ref.shape[1] // side
+    tile_copy = pltpu.make_async_copy(arrived_ref, tiles_ref, tile_sem)
+    tile_copy.start()
 
     def spot(n):
         label = labels_ref[n]
@@ -221,29 +222,35 @@
         def _():
             pltpu.make_async_copy(held.at[n], spot(n), out_sems.at[n]).wait()
 
-    used = lax.fori_loop(0, tiles_ref.shape[0] * slots, fetch, 0)
+    used = lax.fori_loop(0, tiles_ref.shape[0] * slots, fetch, 0, unroll=4)
+    tile_copy.wait()
     for step in (add, put, finish):
         loop(used, step)
 
 
-def place(front, labels, tiles, tile_rows):
+def owners(labels):
+    labels = labels.reshape(-1)
+    ids = jnp.arange(labels.size, dtype=jnp.int32)
+    owner = jnp.min(jnp.where(labels[:, None] == labels[None, :], ids[None, :], labels.size), axis=1)
+    return labels, jnp.where(labels < 0, -1, owner)
+
+
+def place(front, labels, owner, tiles, tile_rows):
     side = tiles.shape[2]
-    labels = labels.reshape(-1)
     size = labels.size
-    ids = jnp.arange(size, dtype=jnp.int32)
-    owner = jnp.min(jnp.where(labels[:, None] == labels[None, :], ids[None, :], size), axis=1)
-    owner = jnp.where(labels < 0, -1, owner)
-    smem = pl.BlockSpec(memory_space=pltpu.SMEM)
+    smem, anyw = (pl.BlockSpec(memory_space=m) for m in (pltpu.SMEM, pl.ANY))
     return pl.pallas_call(
         functools.partial(place_kernel, tile_rows),
         grid=(1,),
         out_shape=jax.ShapeDtypeStruct(front.shape, f32),
-        in_specs=[smem, smem, pl.BlockSpec(tiles.shape, lambda i: (0, 0, 0)), pl.BlockSpec(memory_space=pl.ANY)],
-        out_specs=pl.BlockSpec(memory_space=pl.ANY),
+        in_specs=[smem, smem, anyw, anyw],
+        out_specs=anyw,
         input_output_aliases={3: 0},
         scratch_shapes=[
+            pltpu.VMEM(tiles.shape, bf16),
             pltpu.VMEM((size, side, side), f32),
             pltpu.SMEM((size + 1,), jnp.int32),
+            pltpu.SemaphoreType.DMA,
             pltpu.SemaphoreType.DMA((size,)),
             pltpu.SemaphoreType.DMA((size,)),
         ],
@@ -459,6 +466,20 @@
     labels = head[:, 0].astype(jnp.int32) - 1
     columns, narrow = lead_columns(row[None], labels, frontal, one, tile_rows)
 
+    z, x, c = row // 4, row // 2 % 2, row % 2
+    cols = []
+    for offsets in ([0], [1, layers - 1], list(range(2, layers - 1))):
+        cols += [
+            (z - dz) % layers * 4 + (x ^ dx) * 2 + (c ^ dc) for dc in range(2) for dx in range(2) for dz in offsets
+        ]
+    at = sum(jnp.where(col == 0, g, 0) for g, col in enumerate(cols))
+    info = jnp.stack([row, at] + cols).astype(jnp.int32)
+    wanted = jnp.where(labels % tile_rows < 2, -1, labels)
+    spots = owners(wanted[:, FIRST : FIRST + SECOND])
+    flags = jnp.max(head[:, 1, :2], axis=0)
+    flags = jnp.maximum(flags, lax.ppermute(flags, "groups", [(0, 1), (1, 0)]))
+    case = jnp.where(flags[0] > 0, 2, jnp.where(flags[1] > 0, 1, 0)).astype(jnp.int32)
+
     join = lambda *x: jnp.concatenate(x, axis=0)
     tie = lax.optimization_barrier
     narrow, second = tie((narrow, second))
@@ -467,7 +488,9 @@
     near, beside = join(narrow, over), join(up, down)
     far = [send(narrow, over_z(s)) for s in range(2, layers - 1)]
     beside_x, near_c = send(beside, over_x), send(near, over_core)
-    far, beside_x, near_c, near, beside = tie((far, beside_x, near_c, near, beside))
+    far, beside_x, near_c, near, beside, info, spots, case = tie(
+        (far, beside_x, near_c, near, beside, info, spots, case)
+    )
     far, beside = join(*far), join(beside, beside_x)
     far_x, beside_c = send(far, over_x), send(beside, over_core)
     far_x, beside_c, far = tie((far_x, beside_c, far))
@@ -476,24 +499,10 @@
     far_c, second = tie((far_c, second))
     two = exchange(second)
     parts = [near, near_c, beside, beside_c, far, far_c]
-
-    z, x, c = row // 4, row // 2 % 2, row % 2
-    cols = []
-    for offsets in ([0], [1, layers - 1], list(range(2, layers - 1))):
-        cols += [
-            (z - dz) % layers * 4 + (x ^ dx) * 2 + (c ^ dc) for dc in range(2) for dx in range(2) for dz in offsets
-        ]
-    at = sum(jnp.where(col == 0, g, 0) for g, col in enumerate(cols))
-    info = jnp.stack([row, at] + cols).astype(jnp.int32)
     front = make_front(info, labels, columns, one, frontal, parts, tile_rows)
-
-    wanted = jnp.where(labels % tile_rows < 2, -1, labels)
     front, two = tie((front, two))
-    front = place(front, wanted[:, FIRST : FIRST + SECOND], two, tile_rows)
-    flags = jnp.max(head[:, 1, :2], axis=0)
-    flags = jnp.maximum(flags, lax.ppermute(flags, "groups", [(0, 1), (1, 0)]))
-    front, third, labels = tie((front, third, wanted[:, FIRST + SECOND :]))
-    case = jnp.where(flags[0] > 0, 2, jnp.where(flags[1] > 0, 1, 0)).astype(jnp.int32)
+    front = place(front, *spots, two, tile_rows)
+    front, third, wanted = tie((front, third, wanted[:, FIRST + SECOND :]))
 
     def spread(x, axis):
         every = exchange(jnp.broadcast_to(x[None], (devices,) + x.shape))
@@ -502,11 +511,11 @@
     return lax.switch(
         case,
         [
-            lambda front, third, labels, *args: front,
-            lambda front, third, labels, *args: place(front, labels, exchange(third), tile_rows),
-            lambda front, third, labels, *args: local_small(*args, spread),
+            lambda front, third, wanted, *args: front,
+            lambda front, third, wanted, *args: place(front, *owners(wanted), exchange(third), tile_rows),
+            lambda front, third, wanted, *args: local_small(*args, spread),
         ],
-        front, third, labels, frontal, child_tiles, child_rows, child_cols,
+        front, third, wanted, frontal, child_tiles, child_rows, child_cols,
     )
 
 

time: 154 us -> 148 us (0.961); the launches traced: 154 us -> 145 us
  waiting for transfers between devices: 70.4 us -> 64.3 us
  Pallas kernels: 49.2 us -> 46.8 us
    ppermute x9, waiting for transfers between devices: 36 us -> 31.2 us  [local_fast(): send = lambda x, pairs: lax.ppermute(x, 'row', pairs)]
  transfers between devices with their start and end apart: 12 -> 12, of which waited for: 7 -> 6; matrix products, arithmetic and copies ran while one was open for 1% -> 2% of each run, Pallas kernels for 22% -> 23%
where the time goes in v1:
time: 148 us; the launch traced here: 145 us
  waiting for transfers between devices  64.3 us (43%)
  Pallas kernels  46.8 us (32%)
  starting transfers between devices  26.5 us (18%)
  local copies, waits for them, and re-layouts  4.71 us (3%)
  between operations  1.84 us (1%)
    pallas_call x1, Pallas kernels, make_front(): pl.pallas_call(functools.partial(front_kernel, tile_rows, labels.shape[1]...  33.6 us
    all_to_all x2, waiting for transfers between devices, local_fast(): lax.all_to_all(x, 'row', split_axis=0, concat_axis=0, tiled=True)  33.1 us
    ppermute x9, waiting for transfers between devices, local_fast(): send = lambda x, pairs: lax.ppermute(x, 'row', pairs)  31.2 us
    ppermute x9, starting transfers between devices, local_fast(): send = lambda x, pairs: lax.ppermute(x, 'row', pairs)  13.2 us
    all_to_all x2, starting transfers between devices, local_fast(): lax.all_to_all(x, 'row', split_axis=0, concat_axis=0, tiled=True)  11.8 us
    pallas_call x1, Pallas kernels, pack(): pl.pallas_call(functools.partial(pack_kernel, tile_rows, per_dev), grid=(...  4.86 us
    pallas_call x1, Pallas kernels, place(): pl.pallas_call(functools.partial(place_kernel, tile_rows), grid=(1,), out...  4.18 us
    pallas_call x1, Pallas kernels, lead_columns(): pl.pallas_call(functools.partial(lead_kernel, tile_rows, labels.shape[1])...  4.16 us
  transfers between devices with their start and end apart: 12, of which 6 were waited for; matrix products, arithmetic and copies ran while one was open for 2% of the time, Pallas kernels for 23%

profile of v1, /device:TPU:0, one launch (start us, length us, event | category | flops | bytes accessed | tf_op | source)
XLA Modules:
  0.0 145.2 jit_solution(2321830243927790846)
XLA Ops:
  0.0 4.9 %pack.1 = (bf16[16,400,128]{2,1,0:T(8,128)(2,1)}, bf16[16,384,128]{2,1,0:T(8,128)(2,1)}, bf16[16,256,128]{2,1,0:T(8,128)(2,1)}) custom-call(s32[64]{0:T(128)} %bitcast.103, s32[64]{0:T(128)} %cols_ref.1, bf16[64,128,128]{2,1,0:T(8,128)(2,1)} %tiles_ref.1), custom_call_target="tpu_custom_call" | custom-call | tf_op jit(solution)/shard_map/pack/pallas_call | solution.py:92
  4.9 7.4 %all-to-all-start.4 = ((bf16[16,400,128]{2,1,0:T(8,128)(2,1)}), bf16[16,400,128]{2,1,0:T(8,128)(2,1)S(1)}, u32[]{:S(2)}, u32[]{:S(2)}) async-start(bf16[16,400,128]{2,1,0:T(8,128)(2,1)} %get-tuple-element.88), calls=%async_computation.4 | async-start | bytes 3276800 | tf_op jit(solution)/shard_map/all_to_all | solution.py:461
  12.3 33.1 %all-to-all-done.4.tiles_ref = bf16[16,400,128]{2,1,0:T(8,128)(2,1)S(1)} async-done(((bf16[16,400,128]{2,1,0:T(8,128)(2,1)}), bf16[16,400,128]{2,1,0:T(8,128)(2,1)S(1)}, u32[]{:S(2)}, u32[]{:S(2)}) %all-to-all-start.4) | async-done | bytes 1638432 | tf_op jit(solution)/shard_map/all_to_all | solution.py:461
  45.4 0.0 copy-start.6
  45.4 0.7 sub.62.labels_ref
  46.1 0.4 copy-done.6
  46.5 4.2 %lead_columns.1 = (f32[512,256]{1,0:T(8,128)}, s16[1,272,512]{2,1,0:T(8,128)(2,1)}) custom-call(s32[1]{0:T(128)} %bitcast.20.row_ref, s32[128]{0:T(128)} %sub.62.labels_ref, f32[512,8192]{1,0:T(8,128)} %front_ref.3, bf16[16,400,128]{2,1,0:T(8,128)(2,1)} %copy-done.6), custom_call_target="tpu_custom_call" | custom-call | tf_op jit(solution)/shard_map/lead_columns/pallas_call | solution.py:158
  50.7 5.0 %collective-permute-start = (s16[1,272,512]{2,1,0:T(8,128)(2,1)}, s16[1,272,512]{2,1,0:T(8,128)(2,1)S(1)}, u32[]{:S(2)}, u32[]{:S(2)}) collective-permute-start(s16[1,272,512]{2,1,0:T(8,128)(2,1)} %get-tuple-element.92), channel_id=1, source_target_pairs={{0,4},{1,5},{2,6},{3,7},{4,8},{5,9},{6,10},{7,11},{8,12},{9,13},{1... | collective-permute-start | bytes 835592 | tf_op jit(solution)/shard_map/ppermute | solution.py:460
  55.7 0.0 collective-permute-start.1
  55.7 3.6 %collective-permute-start.2 = (s16[1,272,512]{2,1,0:T(8,128)(2,1)}, s16[1,272,512]{2,1,0:T(8,128)(2,1)S(1)}, u32[]{:S(2)}, u32[]{:S(2)}) collective-permute-start(s16[1,272,512]{2,1,0:T(8,128)(2,1)} %get-tuple-element.92), channel_id=1, source_target_pairs={{0,2},{1,3},{2,0},{3,1},{4,6},{5,7},{6,4},{7,5},{8,10},{9,11},{10,... | collective-permute-start | bytes 835592 | tf_op jit(solution)/shard_map/ppermute | solution.py:460
  59.3 0.6 stack.72.info_ref
  60.0 1.6 %collective-permute-start.6 = (f32[2]{0:T(128)S(1)}, f32[2]{0:T(128)S(1)}, u32[]{:S(2)}, u32[]{:S(2)}) collective-permute-start(f32[2]{0:T(128)S(1)} %slice_reduce_fusion), channel_id=1, source_target_pairs={{0,16},{16,0},{1,17},{17,1},{2,18},{18,2},{3,19},{19,3},{4,20},{20... | collective-permute-start | bytes 32 | tf_op jit(solution)/shard_map/ppermute | solution.py:480
  61.5 0.1 copy.48
  61.6 1.8 %collective-permute-done = s16[1,272,512]{2,1,0:T(8,128)(2,1)S(1)} collective-permute-done((s16[1,272,512]{2,1,0:T(8,128)(2,1)}, s16[1,272,512]{2,1,0:T(8,128)(2,1)S(1)}, u32[]{:S(2)}, u32[]{:S(2)}) %collective-permute-start) | collective-permute-done | bytes 278560 | tf_op jit(solution)/shard_map/ppermute | solution.py:460
  63.4 5.9 %collective-permute-done.1 = s16[1,272,512]{2,1,0:T(8,128)(2,1)S(1)} collective-permute-done((s16[1,272,512]{2,1,0:T(8,128)(2,1)}, s16[1,272,512]{2,1,0:T(8,128)(2,1)S(1)}, u32[]{:S(2)}, u32[]{:S(2)}) %collective-permute-start.1) | collective-permute-done | bytes 278560 | tf_op jit(solution)/shard_map/ppermute | solution.py:460
  69.3 0.0 collective-permute-done.2
  69.3 1.0 constant_dynamic-update-slice_fusion.3
  70.3 0.0 copy-start.11
  70.3 0.1 collective-permute-start.5
  70.4 3.4 %collective-permute-start.4 = (s16[2,272,512]{2,1,0:T(8,128)(2,1)S(1)}, s16[2,272,512]{2,1,0:T(8,128)(2,1)S(1)}, u32[]{:S(2)}, u32[]{:S(2)}) collective-permute-start(s16[2,272,512]{2,1,0:T(8,128)(2,1)S(1)} %constant_dynamic-update-slice_fusion), channel_id=1, source_target_pairs={{0,2},{1,3},{2,0},{3,1},{4,6},{5,7},{6,4},{7,5},{8,10},{9,11},{10,... | collective-permute-start | bytes 1671176 | tf_op jit(solution)/shard_map/ppermute | solution.py:460
  73.8 0.1 copy.49
  73.9 0.1 reshape.189.labels_ref
  74.0 0.0 copy-start.14
  74.0 0.2 select_reduce_fusion.3
  74.2 0.6 collective-permute-start.3
  74.8 0.5 compare_select_fusion.14.owner_ref
  75.4 0.0 collective-permute-done.6
  75.4 0.7 fusion.42
  77.4 12.7 %collective-permute-done.3 = s16[1,272,512]{2,1,0:T(8,128)(2,1)S(1)} collective-permute-done((s16[1,272,512]{2,1,0:T(8,128)(2,1)}, s16[1,272,512]{2,1,0:T(8,128)(2,1)S(1)}, u32[]{:S(2)}, u32[]{:S(2)}) %collective-permute-start.3) | collective-permute-done | bytes 278560 | tf_op jit(solution)/shard_map/ppermute | solution.py:460
  90.1 0.0 collective-permute-done.5.refs_1_
  90.1 0.0 copy-start.13
  90.1 0.0 collective-permute-done.4
  90.1 0.8 copy-done.13
  91.0 0.0 copy-start.9
  91.1 0.1 collective-permute-start.8
  91.1 0.4 collective-permute-start.7
  91.5 8.7 %collective-permute-done.7 = s16[1,272,512]{2,1,0:T(8,128)(2,1)S(1)} collective-permute-done((s16[1,272,512]{2,1,0:T(8,128)(2,1)S(1)}, s16[1,272,512]{2,1,0:T(8,128)(2,1)S(1)}, u32[]{:S(2)}, u32[]{:S(2)}) %collective-permute-start.7) | collective-permute-done | bytes 278560 | tf_op jit(solution)/shard_map/ppermute | solution.py:460
  100.2 0.0 collective-permute-done.8.refs_3_
  100.2 0.0 copy-start.12
  100.3 0.0 copy-start.10
  100.3 0.1 collective-permute-start.9
  100.4 2.1 %collective-permute-done.9.refs_5_ = s16[2,272,512]{2,1,0:T(8,128)(2,1)} collective-permute-done((s16[2,272,512]{2,1,0:T(8,128)(2,1)S(1)}, s16[2,272,512]{2,1,0:T(8,128)(2,1)}, u32[]{:S(2)}, u32[]{:S(2)}) %collective-permute-start.9) | collective-permute-done | bytes 557088 | tf_op jit(solution)/shard_map/ppermute | solution.py:460
  102.4 4.4 %all-to-all-start.5 = ((bf16[16,384,128]{2,1,0:T(8,128)(2,1)}), bf16[16,384,128]{2,1,0:T(8,128)(2,1)}, u32[]{:S(2)}, u32[]{:S(2)}) async-start(bf16[16,384,128]{2,1,0:T(8,128)(2,1)} %get-tuple-element.111), calls=%async_computation.5 | async-start | bytes 3145728 | tf_op jit(solution)/shard_map/all_to_all | solution.py:461
  106.9 0.0 copy-done.11
  106.9 0.0 copy-done.9
  106.9 0.0 copy-done.12
  106.9 0.0 copy-done.10
  106.9 33.6 %front.1.front_ref = f32[512,8192]{1,0:T(8,128)} custom-call(s32[18]{0:T(128)} %stack.72.info_ref, s32[128]{0:T(128)} %sub.62.labels_ref, f32[512,256]{1,0:T(8,128)} %get-tuple-element.100.columns_ref, bf16[16,400,128]{2,1,0:T(8,128)(2,1)} %copy-done.6, f32[512,8192]{1,0:T(8,128)} %front_ref.3, s16[2,272,512]{2,1,0:T(8,128)(2,1)} %copy-done.11, ...), custom_call_target="tpu_custom_call" | custom-call | flops 6442450944 | bytes 33554432 | tf_op jit(solution)/shard_map/front/pallas_call | solution.py:418
  140.5 0.0 copy-done.14
  140.5 0.0 copy-start.7
  140.5 0.0 copy-start.16
  140.6 0.0 copy-start.17
  140.6 0.0 all-to-all-done.5.arrived_ref
  140.6 4.2 %place.3 = f32[512,8192]{1,0:T(8,128)} custom-call(s32[48]{0:T(128)} %copy-done.14, s32[48]{0:T(128)} %compare_select_fusion.14.owner_ref, bf16[16,384,128]{2,1,0:T(8,128)(2,1)} %all-to-all-done.5.arrived_ref, f32[512,8192]{1,0:T(8,128)} %front.1.front_ref), custom_call_target="tpu_custom_call", output_to_operand_aliasing={{}: (3, {})} | custom-call | tf_op jit(solution)/shard_map/place/pallas_call | solution.py:242
  144.8 0.0 copy-done.7
  144.8 0.0 copy-done.16
  144.8 0.0 copy-done.17
  144.8 0.2 conditional.1
  (14 shorter events, 0.3 us)
Async XLA Ops:
  4.9 40.5 %all-to-all-start.4 = ((bf16[16,400,128]{2,1,0:T(8,128)(2,1)}), bf16[16,400,128]{2,1,0:T(8,128)(2,1)S(1)}, u32[]{:S(2)}, u32[]{:S(2)}) async-start(bf16[16,400,128]{2,1,0:T(8,128)(2,1)} %get-tuple-element.88), calls=%async_computation.4 | async-start | bytes 3276800 | tf_op jit(solution)/shard_map/all_to_all | solution.py:461
  45.4 1.2 copy-start.6
  50.7 12.7 %collective-permute-start = (s16[1,272,512]{2,1,0:T(8,128)(2,1)}, s16[1,272,512]{2,1,0:T(8,128)(2,1)S(1)}, u32[]{:S(2)}, u32[]{:S(2)}) collective-permute-start(s16[1,272,512]{2,1,0:T(8,128)(2,1)} %get-tuple-element.92), channel_id=1, source_target_pairs={{0,4},{1,5},{2,6},{3,7},{4,8},{5,9},{6,10},{7,11},{8,12},{9,13},{1... | collective-permute-start | bytes 835592 | tf_op jit(solution)/shard_map/ppermute | solution.py:460
  55.7 13.6 %collective-permute-start.1 = (s16[1,272,512]{2,1,0:T(8,128)(2,1)}, s16[1,272,512]{2,1,0:T(8,128)(2,1)S(1)}, u32[]{:S(2)}, u32[]{:S(2)}) collective-permute-start(s16[1,272,512]{2,1,0:T(8,128)(2,1)} %get-tuple-element.92), channel_id=1, source_target_pairs={{0,12},{1,13},{2,14},{3,15},{4,0},{5,1},{6,2},{7,3},{8,4},{9,5},{1... | collective-permute-start | bytes 835592 | tf_op jit(solution)/shard_map/ppermute | solution.py:460
  55.7 13.6 %collective-permute-start.2 = (s16[1,272,512]{2,1,0:T(8,128)(2,1)}, s16[1,272,512]{2,1,0:T(8,128)(2,1)S(1)}, u32[]{:S(2)}, u32[]{:S(2)}) collective-permute-start(s16[1,272,512]{2,1,0:T(8,128)(2,1)} %get-tuple-element.92), channel_id=1, source_target_pairs={{0,2},{1,3},{2,0},{3,1},{4,6},{5,7},{6,4},{7,5},{8,10},{9,11},{10,... | collective-permute-start | bytes 835592 | tf_op jit(solution)/shard_map/ppermute | solution.py:460
  60.0 15.4 %collective-permute-start.6 = (f32[2]{0:T(128)S(1)}, f32[2]{0:T(128)S(1)}, u32[]{:S(2)}, u32[]{:S(2)}) collective-permute-start(f32[2]{0:T(128)S(1)} %slice_reduce_fusion), channel_id=1, source_target_pairs={{0,16},{16,0},{1,17},{17,1},{2,18},{18,2},{3,19},{19,3},{4,20},{20... | collective-permute-start | bytes 32 | tf_op jit(solution)/shard_map/ppermute | solution.py:480
  70.3 36.6 %copy-start.11 = (s16[2,272,512]{2,1,0:T(8,128)(2,1)}, s16[2,272,512]{2,1,0:T(8,128)(2,1)S(1)}, u32[]{:S(2)}) copy-start(s16[2,272,512]{2,1,0:T(8,128)(2,1)S(1)} %constant_dynamic-update-slice_fusion.2.refs_0_) | copy-start | bytes 1671172
  70.3 19.8 %collective-permute-start.5 = (s16[2,272,512]{2,1,0:T(8,128)(2,1)S(1)}, s16[2,272,512]{2,1,0:T(8,128)(2,1)S(1)}, u32[]{:S(2)}, u32[]{:S(2)}) collective-permute-start(s16[2,272,512]{2,1,0:T(8,128)(2,1)S(1)} %constant_dynamic-update-slice_fusion.2.refs_0_), channel_id=1, source_target_pairs={{0,1},{1,0},{2,3},{3,2},{4,5},{5,4},{6,7},{7,6},{8,9},{9,8},{10,11... | collective-permute-start | bytes 1671176 | tf_op jit(solution)/shard_map/ppermute | solution.py:460
  70.4 19.7 %collective-permute-start.4 = (s16[2,272,512]{2,1,0:T(8,128)(2,1)S(1)}, s16[2,272,512]{2,1,0:T(8,128)(2,1)S(1)}, u32[]{:S(2)}, u32[]{:S(2)}) collective-permute-start(s16[2,272,512]{2,1,0:T(8,128)(2,1)S(1)} %constant_dynamic-update-slice_fusion), channel_id=1, source_target_pairs={{0,2},{1,3},{2,0},{3,1},{4,6},{5,7},{6,4},{7,5},{8,10},{9,11},{10,... | collective-permute-start | bytes 1671176 | tf_op jit(solution)/shard_map/ppermute | solution.py:460
  74.0 66.5 %copy-start.14 = (s32[48]{0:T(128)}, s32[48]{0:T(128)S(1)}, u32[]{:S(2)}) copy-start(s32[48]{0:T(128)S(1)} %reshape.189.labels_ref) | copy-start | bytes 580
  74.2 15.9 %collective-permute-start.3 = (s16[1,272,512]{2,1,0:T(8,128)(2,1)}, s16[1,272,512]{2,1,0:T(8,128)(2,1)S(1)}, u32[]{:S(2)}, u32[]{:S(2)}) collective-permute-start(s16[1,272,512]{2,1,0:T(8,128)(2,1)} %get-tuple-element.92), channel_id=1, source_target_pairs={{0,8},{1,9},{2,10},{3,11},{4,12},{5,13},{6,14},{7,15},{8,0},{9,1},... | collective-permute-start | bytes 835592 | tf_op jit(solution)/shard_map/ppermute | solution.py:460
  90.1 0.9 copy-start.13
  91.0 15.8 %copy-start.9 = (s16[4,272,512]{2,1,0:T(8,128)(2,1)}, s16[4,272,512]{2,1,0:T(8,128)(2,1)S(1)}, u32[]{:S(2)}) copy-start(s16[4,272,512]{2,1,0:T(8,128)(2,1)S(1)} %constant_dynamic-update-slice_fusion.4.refs_2_) | copy-start | bytes 3342340
  91.1 9.2 %collective-permute-start.8 = (s16[4,272,512]{2,1,0:T(8,128)(2,1)S(1)}, s16[4,272,512]{2,1,0:T(8,128)(2,1)S(1)}, u32[]{:S(2)}, u32[]{:S(2)}) collective-permute-start(s16[4,272,512]{2,1,0:T(8,128)(2,1)S(1)} %constant_dynamic-update-slice_fusion.4.refs_2_), channel_id=1, source_target_pairs={{0,1},{1,0},{2,3},{3,2},{4,5},{5,4},{6,7},{7,6},{8,9},{9,8},{10,11... | collective-permute-start | bytes 3342344 | tf_op jit(solution)/shard_map/ppermute | solution.py:460
  91.1 9.1 %collective-permute-start.7 = (s16[1,272,512]{2,1,0:T(8,128)(2,1)S(1)}, s16[1,272,512]{2,1,0:T(8,128)(2,1)S(1)}, u32[]{:S(2)}, u32[]{:S(2)}) collective-permute-start(s16[1,272,512]{2,1,0:T(8,128)(2,1)S(1)} %collective-permute-done.3), channel_id=1, source_target_pairs={{0,2},{1,3},{2,0},{3,1},{4,6},{5,7},{6,4},{7,5},{8,10},{9,11},{10,... | collective-permute-start | bytes 835592 | tf_op jit(solution)/shard_map/ppermute | solution.py:460
  100.2 6.7 %copy-start.12 = (s16[4,272,512]{2,1,0:T(8,128)(2,1)}, s16[4,272,512]{2,1,0:T(8,128)(2,1)S(1)}, u32[]{:S(2)}) copy-start(s16[4,272,512]{2,1,0:T(8,128)(2,1)S(1)} %collective-permute-done.8.refs_3_) | copy-start | bytes 3342340
  100.3 6.6 %copy-start.10 = (s16[2,272,512]{2,1,0:T(8,128)(2,1)}, s16[2,272,512]{2,1,0:T(8,128)(2,1)S(1)}, u32[]{:S(2)}) copy-start(s16[2,272,512]{2,1,0:T(8,128)(2,1)S(1)} %constant_dynamic-update-slice_fusion.6.refs_4_) | copy-start | bytes 1671172
  100.3 2.2 %collective-permute-start.9 = (s16[2,272,512]{2,1,0:T(8,128)(2,1)S(1)}, s16[2,272,512]{2,1,0:T(8,128)(2,1)}, u32[]{:S(2)}, u32[]{:S(2)}) collective-permute-start(s16[2,272,512]{2,1,0:T(8,128)(2,1)S(1)} %constant_dynamic-update-slice_fusion.6.refs_4_), channel_id=1, source_target_pairs={{0,1},{1,0},{2,3},{3,2},{4,5},{5,4},{6,7},{7,6},{8,9},{9,8},{10,11... | collective-permute-start | bytes 1671176 | tf_op jit(solution)/shard_map/ppermute | solution.py:460
  102.4 38.1 %all-to-all-start.5 = ((bf16[16,384,128]{2,1,0:T(8,128)(2,1)}), bf16[16,384,128]{2,1,0:T(8,128)(2,1)}, u32[]{:S(2)}, u32[]{:S(2)}) async-start(bf16[16,384,128]{2,1,0:T(8,128)(2,1)} %get-tuple-element.111), calls=%async_computation.5 | async-start | bytes 3145728 | tf_op jit(solution)/shard_map/all_to_all | solution.py:461
  140.5 4.2 %copy-start.7 = (bf16[64,128,128]{2,1,0:T(8,128)(2,1)S(1)}, bf16[64,128,128]{2,1,0:T(8,128)(2,1)}, u32[]{:S(2)}) copy-start(bf16[64,128,128]{2,1,0:T(8,128)(2,1)} %tiles_ref.1) | copy-start | bytes 6291460
  140.5 4.2 %copy-start.16 = (s32[64,1]{0,1:T(1,128)S(1)}, s32[64,1]{0,1:T(1,128)}, u32[]{:S(2)}) copy-start(s32[64,1]{0,1:T(1,128)} %param.18) | copy-start | bytes 772
  140.6 4.2 %copy-start.17 = (s32[64]{0:T(128)S(1)}, s32[64]{0:T(128)}, u32[]{:S(2)}) copy-start(s32[64]{0:T(128)} %cols_ref.1) | copy-start | bytes 772

commit v2 on v1

--- a/solution.py
+++ b/solution.py
@@ -71,10 +71,9 @@
         return lax.fori_loop(0, devices, lambda d, m: jnp.maximum(m, counts[d]), 0)
 
     loop(tiles, lambda i: place(i, True), 4)
-    lead_over = (most() > FIRST).astype(f32)
+    lead_most = most().astype(f32)
     loop(tiles, lambda i: place(i, False), 4)
-    over = (most() > FIRST + SECOND).astype(f32)
-    flags = jnp.where(lanes == 0, lead_over, jnp.where(lanes == 1, over, 0.0))
+    flags = jnp.where(lanes == 0, lead_most, jnp.where(lanes == 1, most().astype(f32), 0.0))
     marked = jnp.where((subs == 1)[None], flags[None], heads[...])
     heads_out[...] = jnp.concatenate([marked, jnp.zeros_like(marked)], axis=1).astype(bf16)
     copy = pltpu.make_async_copy(heads_out, first_ref.at[:, pl.ds(FIRST * side, HEAD)], head_sem)
@@ -478,7 +477,8 @@
     spots = owners(wanted[:, FIRST : FIRST + SECOND])
     flags = jnp.max(head[:, 1, :2], axis=0)
     flags = jnp.maximum(flags, lax.ppermute(flags, "groups", [(0, 1), (1, 0)]))
-    case = jnp.where(flags[0] > 0, 2, jnp.where(flags[1] > 0, 1, 0)).astype(jnp.int32)
+    case = jnp.where(flags[0] > FIRST, 2, jnp.where(flags[1] > FIRST + SECOND, 1, 0)).astype(jnp.int32)
+    more = flags[1] > FIRST + SECOND + 1
 
     join = lambda *x: jnp.concatenate(x, axis=0)
     tie = lax.optimization_barrier
@@ -488,8 +488,8 @@
     near, beside = join(narrow, over), join(up, down)
     far = [send(narrow, over_z(s)) for s in range(2, layers - 1)]
     beside_x, near_c = send(beside, over_x), send(near, over_core)
-    far, beside_x, near_c, near, beside, info, spots, case = tie(
-        (far, beside_x, near_c, near, beside, info, spots, case)
+    far, beside_x, near_c, near, beside, info, spots, case, more = tie(
+        (far, beside_x, near_c, near, beside, info, spots, case, more)
     )
     far, beside = join(*far), join(beside, beside_x)
     far_x, beside_c = send(far, over_x), send(beside, over_core)
@@ -508,14 +508,25 @@
         every = exchange(jnp.broadcast_to(x[None], (devices,) + x.shape))
         return every.reshape(order, x.shape[1])
 
+    def place_third(front, third, wanted, more, *args):
+        front = place(front, *owners(wanted[:, :1]), exchange(third[:, :side]), tile_rows)
+        if third.shape[1] == side:
+            return front
+        return lax.cond(
+            more,
+            lambda front: place(front, *owners(wanted[:, 1:]), exchange(third[:, side:]), tile_rows),
+            lambda front: front,
+            front,
+        )
+
     return lax.switch(
         case,
         [
-            lambda front, third, wanted, *args: front,
-            lambda front, third, wanted, *args: place(front, *owners(wanted), exchange(third), tile_rows),
-            lambda front, third, wanted, *args: local_small(*args, spread),
+            lambda front, *args: front,
+            place_third,
+            lambda front, third, wanted, more, *args: local_small(*args, spread),
         ],
-        front, third, wanted, frontal, child_tiles, child_rows, child_cols,
+        front, third, wanted, more, frontal, child_tiles, child_rows, child_cols,
     )
 
 

time: 148 us -> 148 us (level)
  no operation moved by 1% of the time
where the time goes in v2:
time: 148 us; the launch traced here: 145 us
  waiting for transfers between devices  63.9 us (43%)
  Pallas kernels  46.9 us (32%)
  starting transfers between devices  26.5 us (18%)
  local copies, waits for them, and re-layouts  4.64 us (3%)
  between operations  2.25 us (2%)
    pallas_call x1, Pallas kernels, make_front(): pl.pallas_call(functools.partial(front_kernel, tile_rows, labels.shape[1]...  33.6 us
    all_to_all x2, waiting for transfers between devices, local_fast(): lax.all_to_all(x, 'row', split_axis=0, concat_axis=0, tiled=True)  33.1 us
    ppermute x9, waiting for transfers between devices, local_fast(): send = lambda x, pairs: lax.ppermute(x, 'row', pairs)  30.8 us
    ppermute x9, starting transfers between devices, local_fast(): send = lambda x, pairs: lax.ppermute(x, 'row', pairs)  13.1 us
    all_to_all x2, starting transfers between devices, local_fast(): lax.all_to_all(x, 'row', split_axis=0, concat_axis=0, tiled=True)  11.8 us
    pallas_call x1, Pallas kernels, pack(): pl.pallas_call(functools.partial(pack_kernel, tile_rows, per_dev), grid=(...  4.87 us
    pallas_call x1, Pallas kernels, place(): pl.pallas_call(functools.partial(place_kernel, tile_rows), grid=(1,), out...  4.2 us
    pallas_call x1, Pallas kernels, lead_columns(): pl.pallas_call(functools.partial(lead_kernel, tile_rows, labels.shape[1])...  4.17 us
  transfers between devices with their start and end apart: 12, of which 6 were waited for; matrix products, arithmetic and copies ran while one was open for 2% of the time, Pallas kernels for 23%

profile of v2, /device:TPU:0, one launch (start us, length us, event | category | flops | bytes accessed | tf_op | source)
XLA Modules:
  0.0 145.3 jit_solution(11803631420845529511)
XLA Ops:
  0.0 4.9 %pack.1 = (bf16[16,400,128]{2,1,0:T(8,128)(2,1)}, bf16[16,384,128]{2,1,0:T(8,128)(2,1)}, bf16[16,256,128]{2,1,0:T(8,128)(2,1)}) custom-call(s32[64]{0:T(128)} %bitcast.112, s32[64]{0:T(128)} %cols_ref.1, bf16[64,128,128]{2,1,0:T(8,128)(2,1)} %tiles_ref.1), custom_call_target="tpu_custom_call" | custom-call | tf_op jit(solution)/shard_map/pack/pallas_call | solution.py:91
  4.9 7.4 %all-to-all-start.5 = ((bf16[16,400,128]{2,1,0:T(8,128)(2,1)}), bf16[16,400,128]{2,1,0:T(8,128)(2,1)S(1)}, u32[]{:S(2)}, u32[]{:S(2)}) async-start(bf16[16,400,128]{2,1,0:T(8,128)(2,1)} %get-tuple-element.105), calls=%async_computation.5 | async-start | bytes 3276800 | tf_op jit(solution)/shard_map/all_to_all | solution.py:460
  12.3 33.1 %all-to-all-done.5.tiles_ref = bf16[16,400,128]{2,1,0:T(8,128)(2,1)S(1)} async-done(((bf16[16,400,128]{2,1,0:T(8,128)(2,1)}), bf16[16,400,128]{2,1,0:T(8,128)(2,1)S(1)}, u32[]{:S(2)}, u32[]{:S(2)}) %all-to-all-start.5) | async-done | bytes 1638432 | tf_op jit(solution)/shard_map/all_to_all | solution.py:460
  45.4 0.0 copy-start.6
  45.4 0.7 sub.62.labels_ref
  46.1 0.4 copy-done.6
  46.6 4.2 %lead_columns.1 = (f32[512,256]{1,0:T(8,128)}, s16[1,272,512]{2,1,0:T(8,128)(2,1)}) custom-call(s32[1]{0:T(128)} %bitcast.22.row_ref, s32[128]{0:T(128)} %sub.62.labels_ref, f32[512,8192]{1,0:T(8,128)} %front_ref.3, bf16[16,400,128]{2,1,0:T(8,128)(2,1)} %copy-done.6), custom_call_target="tpu_custom_call" | custom-call | tf_op jit(solution)/shard_map/lead_columns/pallas_call | solution.py:157
  50.7 5.0 %collective-permute-start = (s16[1,272,512]{2,1,0:T(8,128)(2,1)}, s16[1,272,512]{2,1,0:T(8,128)(2,1)S(1)}, u32[]{:S(2)}, u32[]{:S(2)}) collective-permute-start(s16[1,272,512]{2,1,0:T(8,128)(2,1)} %get-tuple-element.109), channel_id=1, source_target_pairs={{0,4},{1,5},{2,6},{3,7},{4,8},{5,9},{6,10},{7,11},{8,12},{9,13},{1... | collective-permute-start | bytes 835592 | tf_op jit(solution)/shard_map/ppermute | solution.py:459
  55.7 0.0 collective-permute-start.1
  55.7 3.6 %collective-permute-start.2 = (s16[1,272,512]{2,1,0:T(8,128)(2,1)}, s16[1,272,512]{2,1,0:T(8,128)(2,1)S(1)}, u32[]{:S(2)}, u32[]{:S(2)}) collective-permute-start(s16[1,272,512]{2,1,0:T(8,128)(2,1)} %get-tuple-element.109), channel_id=1, source_target_pairs={{0,2},{1,3},{2,0},{3,1},{4,6},{5,7},{6,4},{7,5},{8,10},{9,11},{10,... | collective-permute-start | bytes 835592 | tf_op jit(solution)/shard_map/ppermute | solution.py:459
  59.3 0.6 stack.72.info_ref
  59.9 1.6 %collective-permute-start.6 = (f32[2]{0:T(128)S(1)}, f32[2]{0:T(128)S(1)}, u32[]{:S(2)}, u32[]{:S(2)}) collective-permute-start(f32[2]{0:T(128)S(1)} %slice_reduce_fusion), channel_id=1, source_target_pairs={{0,16},{16,0},{1,17},{17,1},{2,18},{18,2},{3,19},{19,3},{4,20},{20... | collective-permute-start | bytes 32 | tf_op jit(solution)/shard_map/ppermute | solution.py:479
  61.5 0.1 copy.46
  61.6 1.8 %collective-permute-done = s16[1,272,512]{2,1,0:T(8,128)(2,1)S(1)} collective-permute-done((s16[1,272,512]{2,1,0:T(8,128)(2,1)}, s16[1,272,512]{2,1,0:T(8,128)(2,1)S(1)}, u32[]{:S(2)}, u32[]{:S(2)}) %collective-permute-start) | collective-permute-done | bytes 278560 | tf_op jit(solution)/shard_map/ppermute | solution.py:459
  63.4 5.9 %collective-permute-done.1 = s16[1,272,512]{2,1,0:T(8,128)(2,1)S(1)} collective-permute-done((s16[1,272,512]{2,1,0:T(8,128)(2,1)}, s16[1,272,512]{2,1,0:T(8,128)(2,1)S(1)}, u32[]{:S(2)}, u32[]{:S(2)}) %collective-permute-start.1) | collective-permute-done | bytes 278560 | tf_op jit(solution)/shard_map/ppermute | solution.py:459
  69.3 0.0 collective-permute-done.2
  69.3 1.0 constant_dynamic-update-slice_fusion.3
  70.3 0.0 copy-start.12
  70.3 0.1 collective-permute-start.5
  70.5 3.3 %collective-permute-start.4 = (s16[2,272,512]{2,1,0:T(8,128)(2,1)S(1)}, s16[2,272,512]{2,1,0:T(8,128)(2,1)S(1)}, u32[]{:S(2)}, u32[]{:S(2)}) collective-permute-start(s16[2,272,512]{2,1,0:T(8,128)(2,1)S(1)} %constant_dynamic-update-slice_fusion), channel_id=1, source_target_pairs={{0,2},{1,3},{2,0},{3,1},{4,6},{5,7},{6,4},{7,5},{8,10},{9,11},{10,... | collective-permute-start | bytes 1671176 | tf_op jit(solution)/shard_map/ppermute | solution.py:459
  73.8 0.1 copy.47
  73.9 0.1 reshape.194.labels_ref
  74.0 0.0 copy-start.16
  74.0 0.2 select_reduce_fusion.4
  74.2 0.7 collective-permute-start.3
  74.9 0.6 compare_select_fusion.15.owner_ref
  75.4 0.0 collective-permute-done.6
  75.4 0.6 fusion.42
  77.8 12.3 %collective-permute-done.3 = s16[1,272,512]{2,1,0:T(8,128)(2,1)S(1)} collective-permute-done((s16[1,272,512]{2,1,0:T(8,128)(2,1)}, s16[1,272,512]{2,1,0:T(8,128)(2,1)S(1)}, u32[]{:S(2)}, u32[]{:S(2)}) %collective-permute-start.3) | collective-permute-done | bytes 278560 | tf_op jit(solution)/shard_map/ppermute | solution.py:459
  90.1 0.0 collective-permute-done.5.refs_1_
  90.1 0.0 copy-start.15
  90.1 0.0 collective-permute-done.4
  90.1 0.8 copy-done.15
  91.1 0.0 copy-start.8
  91.1 0.1 collective-permute-start.8
  91.2 0.4 collective-permute-start.7
  91.5 8.7 %collective-permute-done.7 = s16[1,272,512]{2,1,0:T(8,128)(2,1)S(1)} collective-permute-done((s16[1,272,512]{2,1,0:T(8,128)(2,1)S(1)}, s16[1,272,512]{2,1,0:T(8,128)(2,1)S(1)}, u32[]{:S(2)}, u32[]{:S(2)}) %collective-permute-start.7) | collective-permute-done | bytes 278560 | tf_op jit(solution)/shard_map/ppermute | solution.py:459
  100.2 0.0 collective-permute-done.8.refs_3_
  100.2 0.0 copy-start.13
  100.3 0.0 copy-start.11
  100.3 0.1 collective-permute-start.9
  100.4 2.1 %collective-permute-done.9.refs_5_ = s16[2,272,512]{2,1,0:T(8,128)(2,1)} collective-permute-done((s16[2,272,512]{2,1,0:T(8,128)(2,1)S(1)}, s16[2,272,512]{2,1,0:T(8,128)(2,1)}, u32[]{:S(2)}, u32[]{:S(2)}) %collective-permute-start.9) | collective-permute-done | bytes 557088 | tf_op jit(solution)/shard_map/ppermute | solution.py:459
  102.4 4.4 %all-to-all-start.6 = ((bf16[16,384,128]{2,1,0:T(8,128)(2,1)}), bf16[16,384,128]{2,1,0:T(8,128)(2,1)}, u32[]{:S(2)}, u32[]{:S(2)}) async-start(bf16[16,384,128]{2,1,0:T(8,128)(2,1)} %get-tuple-element.128), calls=%async_computation.6 | async-start | bytes 3145728 | tf_op jit(solution)/shard_map/all_to_all | solution.py:460
  106.9 0.0 copy-done.12
  106.9 0.0 copy-done.8
  106.9 0.0 copy-done.13
  106.9 0.0 copy-done.11
  106.9 33.6 %front.1.front_ref = f32[512,8192]{1,0:T(8,128)} custom-call(s32[18]{0:T(128)} %stack.72.info_ref, s32[128]{0:T(128)} %sub.62.labels_ref, f32[512,256]{1,0:T(8,128)} %get-tuple-element.117.columns_ref, bf16[16,400,128]{2,1,0:T(8,128)(2,1)} %copy-done.6, f32[512,8192]{1,0:T(8,128)} %front_ref.3, s16[2,272,512]{2,1,0:T(8,128)(2,1)} %copy-done.12, ...), custom_call_target="tpu_custom_call" | custom-call | flops 6442450944 | bytes 33554432 | tf_op jit(solution)/shard_map/front/pallas_call | solution.py:417
  140.5 0.0 copy-done.16
  140.6 0.0 copy-start.7
  140.6 0.0 copy-start.14
  140.6 0.0 copy-start.17
  140.6 0.0 copy-start.18
  140.6 0.0 all-to-all-done.6.arrived_ref
  140.6 4.2 %place.5 = f32[512,8192]{1,0:T(8,128)} custom-call(s32[48]{0:T(128)} %copy-done.16, s32[48]{0:T(128)} %compare_select_fusion.15.owner_ref, bf16[16,384,128]{2,1,0:T(8,128)(2,1)} %all-to-all-done.6.arrived_ref, f32[512,8192]{1,0:T(8,128)} %front.1.front_ref), custom_call_target="tpu_custom_call", output_to_operand_aliasing={{}: (3, {})} | custom-call | tf_op jit(solution)/shard_map/place/pallas_call | solution.py:241
  144.8 0.0 copy-done.7
  144.8 0.0 copy-done.14
  144.8 0.0 copy-done.17
  144.8 0.0 copy-done.18
  144.9 0.2 conditional.2
  (14 shorter events, 0.3 us)
Async XLA Ops:
  4.9 40.5 %all-to-all-start.5 = ((bf16[16,400,128]{2,1,0:T(8,128)(2,1)}), bf16[16,400,128]{2,1,0:T(8,128)(2,1)S(1)}, u32[]{:S(2)}, u32[]{:S(2)}) async-start(bf16[16,400,128]{2,1,0:T(8,128)(2,1)} %get-tuple-element.105), calls=%async_computation.5 | async-start | bytes 3276800 | tf_op jit(solution)/shard_map/all_to_all | solution.py:460
  45.4 1.2 copy-start.6
  50.7 12.7 %collective-permute-start = (s16[1,272,512]{2,1,0:T(8,128)(2,1)}, s16[1,272,512]{2,1,0:T(8,128)(2,1)S(1)}, u32[]{:S(2)}, u32[]{:S(2)}) collective-permute-start(s16[1,272,512]{2,1,0:T(8,128)(2,1)} %get-tuple-element.109), channel_id=1, source_target_pairs={{0,4},{1,5},{2,6},{3,7},{4,8},{5,9},{6,10},{7,11},{8,12},{9,13},{1... | collective-permute-start | bytes 835592 | tf_op jit(solution)/shard_map/ppermute | solution.py:459
  55.7 13.6 %collective-permute-start.1 = (s16[1,272,512]{2,1,0:T(8,128)(2,1)}, s16[1,272,512]{2,1,0:T(8,128)(2,1)S(1)}, u32[]{:S(2)}, u32[]{:S(2)}) collective-permute-start(s16[1,272,512]{2,1,0:T(8,128)(2,1)} %get-tuple-element.109), channel_id=1, source_target_pairs={{0,12},{1,13},{2,14},{3,15},{4,0},{5,1},{6,2},{7,3},{8,4},{9,5},{1... | collective-permute-start | bytes 835592 | tf_op jit(solution)/shard_map/ppermute | solution.py:459
  55.7 13.6 %collective-permute-start.2 = (s16[1,272,512]{2,1,0:T(8,128)(2,1)}, s16[1,272,512]{2,1,0:T(8,128)(2,1)S(1)}, u32[]{:S(2)}, u32[]{:S(2)}) collective-permute-start(s16[1,272,512]{2,1,0:T(8,128)(2,1)} %get-tuple-element.109), channel_id=1, source_target_pairs={{0,2},{1,3},{2,0},{3,1},{4,6},{5,7},{6,4},{7,5},{8,10},{9,11},{10,... | collective-permute-start | bytes 835592 | tf_op jit(solution)/shard_map/ppermute | solution.py:459
  59.9 15.5 %collective-permute-start.6 = (f32[2]{0:T(128)S(1)}, f32[2]{0:T(128)S(1)}, u32[]{:S(2)}, u32[]{:S(2)}) collective-permute-start(f32[2]{0:T(128)S(1)} %slice_reduce_fusion), channel_id=1, source_target_pairs={{0,16},{16,0},{1,17},{17,1},{2,18},{18,2},{3,19},{19,3},{4,20},{20... | collective-permute-start | bytes 32 | tf_op jit(solution)/shard_map/ppermute | solution.py:479
  70.3 36.5 %copy-start.12 = (s16[2,272,512]{2,1,0:T(8,128)(2,1)}, s16[2,272,512]{2,1,0:T(8,128)(2,1)S(1)}, u32[]{:S(2)}) copy-start(s16[2,272,512]{2,1,0:T(8,128)(2,1)S(1)} %constant_dynamic-update-slice_fusion.2.refs_0_) | copy-start | bytes 1671172
  70.3 19.8 %collective-permute-start.5 = (s16[2,272,512]{2,1,0:T(8,128)(2,1)S(1)}, s16[2,272,512]{2,1,0:T(8,128)(2,1)S(1)}, u32[]{:S(2)}, u32[]{:S(2)}) collective-permute-start(s16[2,272,512]{2,1,0:T(8,128)(2,1)S(1)} %constant_dynamic-update-slice_fusion.2.refs_0_), channel_id=1, source_target_pairs={{0,1},{1,0},{2,3},{3,2},{4,5},{5,4},{6,7},{7,6},{8,9},{9,8},{10,11... | collective-permute-start | bytes 1671176 | tf_op jit(solution)/shard_map/ppermute | solution.py:459
  70.5 19.7 %collective-permute-start.4 = (s16[2,272,512]{2,1,0:T(8,128)(2,1)S(1)}, s16[2,272,512]{2,1,0:T(8,128)(2,1)S(1)}, u32[]{:S(2)}, u32[]{:S(2)}) collective-permute-start(s16[2,272,512]{2,1,0:T(8,128)(2,1)S(1)} %constant_dynamic-update-slice_fusion), channel_id=1, source_target_pairs={{0,2},{1,3},{2,0},{3,1},{4,6},{5,7},{6,4},{7,5},{8,10},{9,11},{10,... | collective-permute-start | bytes 1671176 | tf_op jit(solution)/shard_map/ppermute | solution.py:459
  74.0 66.5 %copy-start.16 = (s32[48]{0:T(128)}, s32[48]{0:T(128)S(1)}, u32[]{:S(2)}) copy-start(s32[48]{0:T(128)S(1)} %reshape.194.labels_ref) | copy-start | bytes 580
  74.2 15.9 %collective-permute-start.3 = (s16[1,272,512]{2,1,0:T(8,128)(2,1)}, s16[1,272,512]{2,1,0:T(8,128)(2,1)S(1)}, u32[]{:S(2)}, u32[]{:S(2)}) collective-permute-start(s16[1,272,512]{2,1,0:T(8,128)(2,1)} %get-tuple-element.109), channel_id=1, source_target_pairs={{0,8},{1,9},{2,10},{3,11},{4,12},{5,13},{6,14},{7,15},{8,0},{9,1},... | collective-permute-start | bytes 835592 | tf_op jit(solution)/shard_map/ppermute | solution.py:459
  90.1 0.8 copy-start.15
  91.1 15.8 %copy-start.8 = (s16[4,272,512]{2,1,0:T(8,128)(2,1)}, s16[4,272,512]{2,1,0:T(8,128)(2,1)S(1)}, u32[]{:S(2)}) copy-start(s16[4,272,512]{2,1,0:T(8,128)(2,1)S(1)} %constant_dynamic-update-slice_fusion.4.refs_2_) | copy-start | bytes 3342340
  91.1 9.2 %collective-permute-start.8 = (s16[4,272,512]{2,1,0:T(8,128)(2,1)S(1)}, s16[4,272,512]{2,1,0:T(8,128)(2,1)S(1)}, u32[]{:S(2)}, u32[]{:S(2)}) collective-permute-start(s16[4,272,512]{2,1,0:T(8,128)(2,1)S(1)} %constant_dynamic-update-slice_fusion.4.refs_2_), channel_id=1, source_target_pairs={{0,1},{1,0},{2,3},{3,2},{4,5},{5,4},{6,7},{7,6},{8,9},{9,8},{10,11... | collective-permute-start | bytes 3342344 | tf_op jit(solution)/shard_map/ppermute | solution.py:459
  91.2 9.1 %collective-permute-start.7 = (s16[1,272,512]{2,1,0:T(8,128)(2,1)S(1)}, s16[1,272,512]{2,1,0:T(8,128)(2,1)S(1)}, u32[]{:S(2)}, u32[]{:S(2)}) collective-permute-start(s16[1,272,512]{2,1,0:T(8,128)(2,1)S(1)} %collective-permute-done.3), channel_id=1, source_target_pairs={{0,2},{1,3},{2,0},{3,1},{4,6},{5,7},{6,4},{7,5},{8,10},{9,11},{10,... | collective-permute-start | bytes 835592 | tf_op jit(solution)/shard_map/ppermute | solution.py:459
  100.2 6.7 %copy-start.13 = (s16[4,272,512]{2,1,0:T(8,128)(2,1)}, s16[4,272,512]{2,1,0:T(8,128)(2,1)S(1)}, u32[]{:S(2)}) copy-start(s16[4,272,512]{2,1,0:T(8,128)(2,1)S(1)} %collective-permute-done.8.refs_3_) | copy-start | bytes 3342340
  100.3 6.6 %copy-start.11 = (s16[2,272,512]{2,1,0:T(8,128)(2,1)}, s16[2,272,512]{2,1,0:T(8,128)(2,1)S(1)}, u32[]{:S(2)}) copy-start(s16[2,272,512]{2,1,0:T(8,128)(2,1)S(1)} %constant_dynamic-update-slice_fusion.6.refs_4_) | copy-start | bytes 1671172
  100.3 2.2 %collective-permute-start.9 = (s16[2,272,512]{2,1,0:T(8,128)(2,1)S(1)}, s16[2,272,512]{2,1,0:T(8,128)(2,1)}, u32[]{:S(2)}, u32[]{:S(2)}) collective-permute-start(s16[2,272,512]{2,1,0:T(8,128)(2,1)S(1)} %constant_dynamic-update-slice_fusion.6.refs_4_), channel_id=1, source_target_pairs={{0,1},{1,0},{2,3},{3,2},{4,5},{5,4},{6,7},{7,6},{8,9},{9,8},{10,11... | collective-permute-start | bytes 1671176 | tf_op jit(solution)/shard_map/ppermute | solution.py:459
  102.4 38.2 %all-to-all-start.6 = ((bf16[16,384,128]{2,1,0:T(8,128)(2,1)}), bf16[16,384,128]{2,1,0:T(8,128)(2,1)}, u32[]{:S(2)}, u32[]{:S(2)}) async-start(bf16[16,384,128]{2,1,0:T(8,128)(2,1)} %get-tuple-element.128), calls=%async_computation.6 | async-start | bytes 3145728 | tf_op jit(solution)/shard_map/all_to_all | solution.py:460
  140.6 4.3 %copy-start.7 = (bf16[64,128,128]{2,1,0:T(8,128)(2,1)S(1)}, bf16[64,128,128]{2,1,0:T(8,128)(2,1)}, u32[]{:S(2)}) copy-start(bf16[64,128,128]{2,1,0:T(8,128)(2,1)} %tiles_ref.1) | copy-start | bytes 6291460
  140.6 4.3 %copy-start.14 = (bf16[16,256,128]{2,1,0:T(8,128)(2,1)S(1)}, bf16[16,256,128]{2,1,0:T(8,128)(2,1)}, u32[]{:S(2)}) copy-start(bf16[16,256,128]{2,1,0:T(8,128)(2,1)} %get-tuple-element.135) | copy-start | bytes 3145732
  140.6 4.3 %copy-start.17 = (s32[64,1]{0,1:T(1,128)S(1)}, s32[64,1]{0,1:T(1,128)}, u32[]{:S(2)}) copy-start(s32[64,1]{0,1:T(1,128)} %param.20) | copy-start | bytes 772
  140.6 4.3 %copy-start.18 = (s32[64]{0:T(128)S(1)}, s32[64]{0:T(128)}, u32[]{:S(2)}) copy-start(s32[64]{0:T(128)} %cols_ref.1) | copy-start | bytes 772
